TPU v7x, 512 devices: a whole 4x8x8 slice. The times are simulated.
512 devices in a mesh: group: 128 (over z, y, x_lo), bank: 4 (over x_hi, core).
Axes of the slice: x: 4 (x_hi: 2, x_lo: 2; x = x_hi * 2 + x_lo), y: 8, z: 8, core: 2. Of those that a mesh axis runs over, the one named last changes fastest.
Arguments:
- traces: bfloat16 [384, 131072], P('group'), may hold values from -127 to 127
- scales: float32 [384, 512], P('group'), may hold values from 0.004 to 0.04
- templates: bfloat16 [4, 128, 16, 128, 384], P('bank', 'group'), may hold values from -0.02734375 to 0.02734375
- owners: int32 [2, 4], P(None, 'bank'), may hold values from 0 to 127
Outputs:
- scores: float32 [2, 4, 16, 131072], P(None, 'bank', None, 'group')
- best_score: float32 [131072], P('group')
All inputs are finite; a program needn't handle non-finite values.
Results may differ from a plain program's by a relative error of at most 0.0029.
Values may be sent and summed in bfloat16 or wider, within the bound.
No kernel may reach another device: no remote copies, remote signals or barrier semaphores. Data moves between devices by JAX's collectives and lax.ppermute only.
A program may use at most 128 MiB of HBM per device.

v0:
```python
import jax
import jax.numpy as jnp
from jax import lax
from jax.sharding import PartitionSpec as P

TLEN = 128
STEPS = 2


def spread(array, axis, root):
    mine = lax.axis_index(axis) == root
    return lax.psum(jnp.where(mine, array, jnp.zeros_like(array)), axis)


def passed_along(block, axis, distance):
    devices = range(lax.axis_size(axis))
    route = [(i - distance, i) for i in devices if i - distance in devices]
    return lax.ppermute(block, axis, route)


def fetch(templates, owners, step_idx):
    root_dev = owners[step_idx, 0]
    received = spread(templates[0, 0], "group", root_dev)
    return received[:, ::-1, :]


def regroup_blocks(windows):
    width_all = windows.shape[2]
    arrived = lax.all_to_all(windows, "group", split_axis=1, concat_axis=0, tiled=True)
    return arrived.reshape(arrived.shape[0], width_all)


def correlate(tmpl_block, extended, span_len):
    num_rows = tmpl_block.shape[0]
    num_lags = tmpl_block.shape[1]
    matrix = tmpl_block.reshape(num_rows * num_lags, tmpl_block.shape[2])
    tile_len = min(1024, span_len)
    width_all = tile_len + num_lags

    def one_tile(tile_id):
        product = jnp.dot(matrix, extended, preferred_element_type=jnp.float32)
        flat_view = product.reshape(num_rows, num_lags * width_all)[:, : num_lags * (width_all - 1)]
        skewed = flat_view.reshape(num_rows, num_lags, width_all - 1)
        return jnp.sum(skewed[:, :, num_lags - 1 : num_lags - 1 + tile_len], axis=1)

    pieces = lax.map(one_tile, jnp.arange(span_len // tile_len, dtype=jnp.int32))
    return pieces.transpose(1, 0, 2).reshape(num_rows, span_len)


def body(traces, scales, templates, owners):
    devices = lax.axis_size("group")
    station_ch, samples_all = traces.shape
    span_len = samples_all // devices
    blocked = traces.astype(jnp.float32).reshape(station_ch, scales.shape[1], -1)
    samples = (blocked * scales[:, :, None]).reshape(station_ch, samples_all).astype(jnp.bfloat16)
    by_block = samples.reshape(station_ch, devices, span_len)
    local_part = regroup_blocks(by_block)
    rim_cells = passed_along(local_part[:, :TLEN], "group", -1)
    extended = jnp.concatenate([local_part, rim_cells], axis=1)
    scores = jnp.stack(
        [
            correlate(fetch(templates, owners, step_idx), extended, span_len)
            for step_idx in range(STEPS)
        ]
    )[:, None]
    local_peak = jnp.max(scores, axis=(0, 1, 2))
    best_score = lax.pmax(local_peak, "bank")
    return (scores, best_score)


def solution(mesh):
    placed = (
        P("group", None),
        P("group", None),
        P("bank", "group", None, None, None),
        P(None, "bank"),
    )
    return jax.shard_map(
        body,
        mesh=mesh,
        in_specs=placed,
        out_specs=(P(None, "bank", None, "group"), P("group")),
        check_vma=False,
    )
```

profile of v0, /device:TPU:1, one launch (start us, length us, event | category | flops | bytes accessed | tf_op | source)
XLA Modules:
  0.0 1375.5 jit_solution(4046613894723460854)
XLA Ops:
  7.2 1.3 fusion
  9.8 1.7 select_bitcast_fusion.1
  11.5 15.3 %rev.6 = bf16[16,128,384]{2,1,0:T(8,128)(2,1)} reverse(bf16[16,128,384]{2,1,0:T(8,128)(2,1)S(1)} %get-tuple-element.24), dimensions={1} | reverse | bytes 3145728 | tf_op jit(solution)/shard_map/rev | solution.py:24
  26.8 15.2 %rev.7 = bf16[16,128,384]{2,1,0:T(8,128)(2,1)} reverse(bf16[16,128,384]{2,1,0:T(8,128)(2,1)S(1)} %get-tuple-element.25), dimensions={1} | reverse | bytes 3145728 | tf_op jit(solution)/shard_map/rev | solution.py:24
  42.0 0.3 broadcast_bitcast_fusion
  42.3 1.1 copy.7
  43.5 0.5 multiply_convert_fusion
  44.0 46.3 %all_to_all.15 = bf16[3,128,1024]{2,0,1:T(4,128)(2,1)S(1)} all-to-all(bf16[3,128,1024]{2,0,1:T(4,128)(2,1)S(1)} %bitcast.29), channel_id=1, replica_groups=mesh['group'=128,'bank'=4] {'group'}, dimensions={1} | all-to-all | bytes 1572864 | tf_op jit(solution)/shard_map/all_to_all | solution.py:29
  90.3 0.7 reshape.45
  91.1 1.3 collective-permute-start
  92.4 4.7 collective-permute-done
  97.1 1072.2 %all-reduce.3.cloned.1.call-done = (bf16[2048,384]{1,0:T(8,128)(2,1)}, bf16[2048,384]{1,0:T(8,128)(2,1)}) async-done(((bf16[2048,384]{1,0:T(8,128)(2,1)}, bf16[2048,384]{1,0:T(8,128)(2,1)}), (bf16[2048,384]{1,0:T(8,128)(2,1)}, bf16[2048,384]{1,0:T(8,128)(2,1)})) %all-reduce.3.cloned.1.call-update) | async-done | bytes 3145744 | tf_op jit(solution)/shard_map/psum | solution.py:12
  1169.3 7.8 fusion.2
  1177.0 10.6 reshape.49
  1187.7 6.6 slice.35
  1194.3 19.4 %reshape.50 = f32[16,128,1151]{2,1,0:T(8,128)} reshape(f32[16,147328]{1,0:T(8,128)} %slice.35) | data formatting | bytes 18857984 | tf_op jit(solution)/shard_map/while/body/eval_jaxpr/reshape | solution.py:43
  1213.7 6.0 slice_reduce_fusion
  1219.7 5.1 fusion.1
  1224.9 10.6 reshape.46
  1235.5 6.7 slice.33
  1242.1 19.4 %reshape.47 = f32[16,128,1151]{2,1,0:T(8,128)} reshape(f32[16,147328]{1,0:T(8,128)} %slice.33) | data formatting | bytes 18857984 | tf_op jit(solution)/shard_map/while/body/eval_jaxpr/reshape | solution.py:43
  1261.5 5.9 slice_reduce_fusion.1
  1267.5 100.5 %pmax.7 = f32[1024]{0:T(1024)} all-reduce(f32[1024]{0:T(1024)S(1)} %reduce_max.19), channel_id=1, replica_groups=mesh['group'=128,'bank'=4] {'bank'}, use_global_device_ids=true, to_apply=%region_6.7 | all-reduce | flops 1024 | bytes 8192 | tf_op jit(solution)/shard_map/pmax | solution.py:67
  1368.0 0.7 maximum_bitcast_fusion
  (16 shorter events, 0.3 us)
Async XLA Ops:
  7.2 34.8 %copy-start = (f32[3,512]{1,0:T(4,128)S(1)}, f32[3,512]{1,0:T(4,128)}, u32[]{:S(2)}) copy-start(f32[3,512]{1,0:T(4,128)} %param.5) | copy-start | bytes 18436
  7.2 1162.1 %all-reduce.3.cloned.1.call-start = ((), (), s32[]{:S(2)}) async-start(), calls=%async_computation.1 | async-start | bytes 6291456 | tf_op jit(solution)/shard_map/psum | solution.py:12
  42.2 1.2 copy-start.3
  91.1 6.0 collective-permute-start
  1213.7 6.0 copy-start.2
  1261.5 107.1 %copy-start.1 = (f32[3,512]{1,0:T(4,128)S(1)}, f32[3,512]{1,0:T(4,128)}, u32[]{:S(2)}) copy-start(f32[3,512]{1,0:T(4,128)} %param.5) | copy-start | bytes 18436
Sparse Core Ops, SparseCore 0:
  42.1 1127.1 all-reduce.2
where the time goes:
time: 1380 us
  waiting for transfers between devices  1080 us (78%)
  blocking collectives  147 us (11%)
  local copies, waits for them, and re-layouts  107 us (8%)
  between operations  15.5 us (1%)
  other arithmetic  14.9 us (1%)
    psum x1, waiting for transfers between devices, spread(): return lax.psum(jnp.where(mine, array, jnp.zeros_like(array)), axis)  1070 us
    pmax x1, blocking collectives, body(): best_score = lax.pmax(local_peak, 'bank')  100 us
    all_to_all x1, blocking collectives, regroup_blocks(): lax.all_to_all(windows, 'group', split_axis=1, concat_axis=0, tiled=True)  46.3 us
    reshape x2, local copies, waits for them, and re-layouts, one_tile(): skewed = flat_view.reshape(num_rows, num_lags, width_all - 1)  38.7 us
    rev x2, local copies, waits for them, and re-layouts, fetch(): return received[:, ::-1, :]  30.4 us
  transfers between devices with their start and end apart: 2, of which 2 were waited for; matrix products, arithmetic and copies ran while one was open for 0% of the time, Pallas kernels for 0%

commit v1 on v0

v1 whole, which is shorter than its diff:
```python
import jax
import jax.numpy as jnp
from jax import lax
from jax.experimental import pallas as pl
from jax.experimental.pallas import tpu as pltpu
from jax.sharding import PartitionSpec as P

TLEN = 128
STEPS = 2
TPL = 16
CH = 384
TIME_DEV = 1024
LANES = 128

HI = 4
CUBES = 16
CLASSES = 8
STATION = 3
CLASS_CH = CUBES * STATION
SHIFTS = TLEN // 16
RUN_ROWS = 33
RUN = RUN_ROWS * LANES
SPAN = 4 * TIME_DEV
PIECE = TPL * CH // LANES
SAMPLE_ROWS = 208
SEND_ROWS = STEPS * PIECE + SAMPLE_ROWS
VMEM = pltpu.CompilerParams(vmem_limit_bytes=56 * 1024 * 1024)


def group_index(cube, klass):
    z_hi, y_hi = divmod(cube, HI)
    z_lo, low = divmod(klass, 4)
    return z_hi * 32 + z_lo * 16 + y_hi * 4 + low


CLASS_GROUPS = [[group_index(cube, klass) for cube in range(CUBES)] for klass in range(CLASSES)]
CUBE_GROUPS = [[group_index(cube, klass) for klass in range(CLASSES)] for cube in range(CUBES)]


def iota(shape, axis):
    return lax.broadcasted_iota(jnp.int32, shape, axis)


def matmul(left, right):
    return jnp.dot(left, right, preferred_element_type=jnp.float32)


def one_hot(flags):
    return jnp.where(flags, 1.0, 0.0).astype(jnp.bfloat16)


def split_kernel(block_ref, out_ref, sorted_ref):
    channel = iota((CH, 1), 0)
    station = channel // STATION
    cube = (station // 32) * HI + (station // 4) % HI
    klass = ((station // 16) % 2) * 4 + station % 4
    target = klass * LANES + (channel % STATION) * CUBES + cube
    by_class = one_hot(iota((CH, CLASSES * LANES), 1) == target)
    for shift in range(SHIFTS):
        rows = block_ref[:, shift * 16 : shift * 16 + 16, :].reshape(TPL * 16, CH)
        parted = matmul(rows, by_class).astype(jnp.bfloat16)
        for klass_id in range(CLASSES):
            sorted_ref[klass_id, :, shift * LANES : (shift + 1) * LANES] = parted[
                :, klass_id * LANES : (klass_id + 1) * LANES
            ]
    padded = iota((SHIFTS * LANES, 1), 0)
    lane = padded % LANES
    target = jnp.where(lane < CLASS_CH, (padded // LANES) * CLASS_CH + lane, -1)
    dense = one_hot(iota((SHIFTS * LANES, CH), 1) == target)
    for klass_id in range(CLASSES):
        packed = matmul(sorted_ref[klass_id], dense).astype(jnp.bfloat16)
        for cube_id in range(CUBES):
            for tile in range(CH // LANES):
                out_ref[group_index(cube_id, klass_id), tile * 16 : tile * 16 + 16, :] = packed[
                    cube_id * 16 : cube_id * 16 + 16, tile * LANES : (tile + 1) * LANES
                ]


def split_block(block):
    return pl.pallas_call(
        split_kernel,
        out_shape=jax.ShapeDtypeStruct((CUBES * CLASSES, PIECE, LANES), jnp.bfloat16),
        in_specs=[pl.BlockSpec(memory_space=pltpu.VMEM)],
        out_specs=pl.BlockSpec(memory_space=pltpu.VMEM),
        scratch_shapes=[pltpu.VMEM((CLASSES, TPL * 16, SHIFTS * LANES), jnp.bfloat16)],
        compiler_params=VMEM,
        cost_estimate=pl.CostEstimate(flops=3_200_000_000, bytes_accessed=3 << 20, transcendentals=0),
        name="split_block",
    )(block)


def pack_kernel(owners_ref, first_ref, second_ref, samples_ref, out_ref, wide_ref, stage_ref):
    wide_ref[:, 0:1024, :] = samples_ref[...].astype(jnp.float32)
    wide_ref[:, 1024:, :] = jnp.zeros((STATION, 8, LANES), jnp.float32)
    first = first_ref[0]
    second = second_ref[0]
    for cube in range(CUBES):
        z_hi, y_hi = divmod(cube, HI)
        out_ref[cube, 0:PIECE, :] = first
        out_ref[cube, PIECE : 2 * PIECE, :] = second
        for z_lo in range(2):
            for ch in range(STATION):
                start = z_hi * 256 + z_lo * 128 + y_hi * 32
                at = (z_lo * STATION + ch) * RUN_ROWS
                stage_ref[at : at + RUN_ROWS, :] = wide_ref[ch, start : start + RUN_ROWS, :]
        stage_ref[6 * RUN_ROWS :, :] = jnp.zeros((SAMPLE_ROWS - 6 * RUN_ROWS, LANES), jnp.float32)
        out_ref[cube, 2 * PIECE :, :] = stage_ref[...].astype(jnp.bfloat16)


def pack(owners, pieces, samples):
    spec = pltpu.PrefetchScalarGridSpec(
        num_scalar_prefetch=1,
        grid=(1,),
        in_specs=[
            pl.BlockSpec((1, PIECE, LANES), lambda i, owners: (owners[0], 0, 0)),
            pl.BlockSpec((1, PIECE, LANES), lambda i, owners: (owners[1], 0, 0)),
            pl.BlockSpec((STATION, 1024, LANES), lambda i, owners: (0, 0, 0)),
        ],
        out_specs=pl.BlockSpec((CUBES, SEND_ROWS, LANES), lambda i, owners: (0, 0, 0)),
        scratch_shapes=[
            pltpu.VMEM((STATION, 1032, LANES), jnp.float32),
            pltpu.VMEM((SAMPLE_ROWS, LANES), jnp.float32),
        ],
    )
    return pl.pallas_call(
        pack_kernel,
        grid_spec=spec,
        out_shape=jax.ShapeDtypeStruct((CUBES, SEND_ROWS, LANES), jnp.bfloat16),
        compiler_params=VMEM,
        cost_estimate=pl.CostEstimate(flops=1_000_000, bytes_accessed=2 << 20, transcendentals=0),
        name="pack",
    )(owners, pieces, pieces, samples)


def correlate_kernel(recv_ref, out_ref, stage_ref, natural_ref, weight_ref, x_ref, product_ref):
    for cube in range(CUBES):
        for step in range(STEPS):
            for tile in range(CH // LANES):
                at = step * PIECE + tile * 16
                natural_ref[(cube * STEPS + step) * 16 : (cube * STEPS + step + 1) * 16, tile * LANES : (tile + 1) * LANES] = (
                    recv_ref[cube, at : at + 16, :]
                )
        stage_ref[cube * SAMPLE_ROWS : (cube + 1) * SAMPLE_ROWS, :] = recv_ref[cube, 2 * PIECE :, :].astype(jnp.float32)
    rows = TPL * STEPS * 16
    wanted = iota((rows, 1), 0)
    lag, step, template = wanted // 32, (wanted // 16) % 2, wanted % 16
    order = one_hot(iota((rows, rows), 1) == (template * 2 + step) * 16 + lag)
    weight_ref[...] = matmul(order, natural_ref[...]).astype(jnp.bfloat16)
    for run in range(2):
        for ch in range(STATION):
            pieces = []
            for block in range(RUN_ROWS):
                at = (run * STATION + ch) * RUN_ROWS + block
                pieces.append(stage_ref[pl.ds(at, CUBES, stride=SAMPLE_ROWS), :])
            line = jnp.concatenate(pieces, axis=1)
            for shift in range(SHIFTS):
                moved = line if shift == 0 else pltpu.roll(line, RUN - 16 * shift, 1)
                at = shift * CLASS_CH + ch * CUBES
                x_ref[at : at + CUBES, :] = moved.astype(jnp.bfloat16)
        for start in range(0, RUN, 1408):
            product_ref[:, start : start + 1408] = matmul(weight_ref[...], x_ref[:, start : start + 1408])
        for part in range(4):
            total = product_ref[0:32, part * TIME_DEV : (part + 1) * TIME_DEV]
            for lag in range(1, 16):
                window = product_ref[lag * 32 : (lag + 1) * 32, part * TIME_DEV : (part + 1) * TIME_DEV + LANES]
                total = total + pltpu.roll(window, TIME_DEV + LANES - lag, 1)[:, :TIME_DEV]
            out_ref[run * 4 + part] = total


def correlate(received):
    return pl.pallas_call(
        correlate_kernel,
        out_shape=jax.ShapeDtypeStruct((CLASSES, STEPS * TPL, TIME_DEV), jnp.float32),
        in_specs=[pl.BlockSpec(memory_space=pltpu.VMEM)],
        out_specs=pl.BlockSpec(memory_space=pltpu.VMEM),
        scratch_shapes=[
            pltpu.VMEM((CUBES * SAMPLE_ROWS, LANES), jnp.float32),
            pltpu.VMEM((TPL * STEPS * 16, CH), jnp.bfloat16),
            pltpu.VMEM((TPL * STEPS * 16, CH), jnp.bfloat16),
            pltpu.VMEM((CH, RUN), jnp.bfloat16),
            pltpu.VMEM((TPL * STEPS * 16, RUN), jnp.float32),
        ],
        compiler_params=VMEM,
        cost_estimate=pl.CostEstimate(flops=3_400_000_000, bytes_accessed=3 << 20, transcendentals=0),
        name="correlate",
    )(received)


def body(traces, scales, templates, owners):
    station_ch, samples_all = traces.shape
    blocked = traces.astype(jnp.float32).reshape(station_ch, scales.shape[1], -1)
    samples = (blocked * scales[:, :, None]).astype(jnp.bfloat16).reshape(station_ch, samples_all // LANES, LANES)
    pieces = split_block(templates[0, 0])
    pieces = lax.all_to_all(pieces, "group", 0, 0, tiled=True)
    sent = pack(owners[:, 0], pieces, samples)
    received = lax.all_to_all(sent, "group", 0, 0, axis_index_groups=CLASS_GROUPS, tiled=True)
    partial = correlate(received)
    partial = lax.all_to_all(partial, "group", 0, 0, axis_index_groups=CUBE_GROUPS, tiled=True)
    scores = jnp.sum(partial, axis=0).reshape(STEPS, 1, TPL, TIME_DEV)
    best_score = lax.pmax(jnp.max(scores, axis=(0, 1, 2)), "bank")
    return (scores, best_score)


def solution(mesh):
    placed = (
        P("group", None),
        P("group", None),
        P("bank", "group", None, None, None),
        P(None, "bank"),
    )
    return jax.shard_map(
        body,
        mesh=mesh,
        in_specs=placed,
        out_specs=(P(None, "bank", None, "group"), P("group")),
        check_vma=False,
    )
```

time: 1380 us -> 153 us (0.11)
  waiting for transfers between devices: 1080 us -> 34.4 us
  local copies, waits for them, and re-layouts: 107 us -> 2.37 us
  blocking collectives: 147 us -> 72 us
  Pallas kernels: 0 us -> 21.4 us
  starting transfers between devices: 1.33 us -> 19.4 us
  between operations: 15.5 us -> 0.69 us
    psum x1 -> x0, waiting for transfers between devices: 1070 us -> none  [spread(): return lax.psum(jnp.where(mine, array, jnp.zeros_like(array)), axis)]
    pmax x1, blocking collectives: 100 us -> 9.56 us  [body(): best_score = lax.pmax(jnp.max(scores, axis=(0, 1, 2)), 'bank')]
    reshape x5 -> x0, local copies, waits for them, and re-layouts: 60.6 us -> none  [the longest x2 38.7 us: one_tile(): skewed = flat_view.reshape(num_rows, num_lags, width_all - 1)]
    all_to_all x0 -> x1, waiting for transfers between devices: none -> 34.4 us  [body(): pieces = lax.all_to_all(pieces, 'group', 0, 0, tiled=True)]
    rev x2 -> x0, local copies, waits for them, and re-layouts: 30.4 us -> none  [fetch(): return received[:, ::-1, :]]
    pallas_call x0 -> x3, Pallas kernels: none -> 21.4 us  [the longest x1 10.3 us: correlate(): pl.pallas_call(correlate_kernel, out_shape=jax.ShapeDtypeStruct((CLASSES,...]
    all_to_all x0 -> x1, starting transfers between devices: none -> 19.4 us  [body(): pieces = lax.all_to_all(pieces, 'group', 0, 0, tiled=True)]
    all_to_all x1 -> x2, blocking collectives: 46.3 us -> 62.5 us  [the longest x1 43.2 us: body(): lax.all_to_all(sent, 'group', 0, 0, axis_index_groups=CLASS_GROUPS, tiled...]
  transfers between devices with their start and end apart: 2 -> 1, of which waited for: 2 -> 1; matrix products, arithmetic and copies ran while one was open for 0% -> 2% of each run, Pallas kernels for 0% -> 0%
where the time goes in v1:
time: 153 us; the launch traced here: 152 us
  blocking collectives  72 us (47%)
  waiting for transfers between devices  34.4 us (22%)
  Pallas kernels  21.4 us (14%)
  starting transfers between devices  19.4 us (13%)
  local copies, waits for them, and re-layouts  2.37 us (2%)
  other arithmetic  1.69 us (1%)
    all_to_all x1, blocking collectives, body(): lax.all_to_all(sent, 'group', 0, 0, axis_index_groups=CLASS_GROUPS, tiled...  43.2 us
    all_to_all x1, waiting for transfers between devices, body(): pieces = lax.all_to_all(pieces, 'group', 0, 0, tiled=True)  34.4 us
    all_to_all x1, starting transfers between devices, body(): pieces = lax.all_to_all(pieces, 'group', 0, 0, tiled=True)  19.4 us
    all_to_all x1, blocking collectives, body(): lax.all_to_all(partial, 'group', 0, 0, axis_index_groups=CUBE_GROUPS, til...  19.3 us
    pallas_call x1, Pallas kernels, correlate(): pl.pallas_call(correlate_kernel, out_shape=jax.ShapeDtypeStruct((CLASSES,...  10.3 us
    pmax x1, blocking collectives, body(): best_score = lax.pmax(jnp.max(scores, axis=(0, 1, 2)), 'bank')  9.56 us
    pallas_call x1, Pallas kernels, split_block(): pl.pallas_call(split_kernel, out_shape=jax.ShapeDtypeStruct((CUBES * CLAS...  7.83 us
    pallas_call x1, Pallas kernels, pack(): pl.pallas_call(pack_kernel, grid_spec=spec, out_shape=jax.ShapeDtypeStruc...  3.25 us
  transfers between devices with their start and end apart: 1, of which 1 were waited for; matrix products, arithmetic and copies ran while one was open for 2% of the time, Pallas kernels for 0%

profile of v1, /device:TPU:1, one launch (start us, length us, event | category | flops | bytes accessed | tf_op | source)
XLA Modules:
  0.0 152.0 jit_solution(16629860988481652912)
XLA Ops:
  0.6 7.8 %split_block.1 = bf16[128,48,128]{2,1,0:T(8,128)(2,1)} custom-call(bf16[16,128,384]{2,1,0:T(8,128)(2,1)} %bitcast.11), custom_call_target="tpu_custom_call" | custom-call | flops 3200000000 | bytes 3145728 | tf_op jit(solution)/shard_map/split_block/pallas_call | solution.py:80
  8.5 0.0 copy-start.3
  8.5 19.4 %all-to-all-start = ((bf16[128,48,128]{2,1,0:T(8,128)(2,1)}), bf16[128,48,128]{2,1,0:T(8,128)(2,1)S(1)}, u32[]{:S(2)}, u32[]{:S(2)}) async-start(bf16[128,48,128]{2,1,0:T(8,128)(2,1)} %split_block.1), calls=%async_computation | async-start | bytes 3145728 | tf_op jit(solution)/shard_map/all_to_all | solution.py:194
  27.9 0.0 copy-done.3
  27.9 0.0 copy-start.1
  27.9 0.3 mul.13
  28.2 0.5 mul.14
  28.6 0.5 copy-done.1
  29.1 0.2 convert_bitcast_fusion
  29.4 1.4 fusion.samples_ref
  30.7 34.4 %all-to-all-done.first_ref.second_ref = bf16[128,48,128]{2,1,0:T(8,128)(2,1)S(1)} async-done(((bf16[128,48,128]{2,1,0:T(8,128)(2,1)}), bf16[128,48,128]{2,1,0:T(8,128)(2,1)S(1)}, u32[]{:S(2)}, u32[]{:S(2)}) %all-to-all-start) | async-done | bytes 1572896 | tf_op jit(solution)/shard_map/all_to_all | solution.py:194
  65.1 0.0 copy-start
  65.1 1.2 copy-done
  66.3 3.3 %pack.1 = bf16[16,304,128]{2,1,0:T(8,128)(2,1)} custom-call(s32[2]{0:T(128)} %bitcast.10, bf16[128,48,128]{2,1,0:T(8,128)(2,1)} %copy-done, bf16[128,48,128]{2,1,0:T(8,128)(2,1)} %copy-done, bf16[3,1024,128]{2,1,0:T(8,128)(2,1)} %fusion.samples_ref), custom_call_target="tpu_custom_call" | custom-call | flops 1000000 | bytes 2097152 | tf_op jit(solution)/shard_map/pack/pallas_call | solution.py:125
  69.5 43.2 %all_to_all.15.recv_ref = bf16[16,304,128]{2,1,0:T(8,128)(2,1)} all-to-all(bf16[16,304,128]{2,1,0:T(8,128)(2,1)} %pack.1), channel_id=1, replica_groups={{0,16,32,48,128,144,160,176,256,272,288,304,384,400,416,432},{4,20,36,5..., dimensions={0} | all-to-all | bytes 2490368 | tf_op jit(solution)/shard_map/all_to_all | solution.py:196
  112.8 10.3 %correlate.1 = f32[8,32,1024]{2,1,0:T(8,128)} custom-call(bf16[16,304,128]{2,1,0:T(8,128)(2,1)} %all_to_all.15.recv_ref), custom_call_target="tpu_custom_call" | custom-call | flops 3400000000 | bytes 3145728 | tf_op jit(solution)/shard_map/correlate/pallas_call | solution.py:171
  123.1 19.3 %all_to_all.16 = f32[8,32,1024]{2,1,0:T(8,128)S(1)} all-to-all(f32[8,32,1024]{2,1,0:T(8,128)} %correlate.1), channel_id=1, replica_groups={{0,4,8,12,64,68,72,76},{16,20,24,28,80,84,88,92},{32,36,40,44,96,100,10..., dimensions={0} | all-to-all | bytes 2097152 | tf_op jit(solution)/shard_map/all_to_all | solution.py:198
  142.4 0.1 reduce_sum.9
  142.4 0.0 copy-start.2
  142.5 9.6 %pmax.7 = f32[1024]{0:T(1024)} all-reduce(f32[1024]{0:T(1024)S(1)} %reduce_max.9), channel_id=1, replica_groups=mesh['group'=128,'bank'=4] {'bank'}, use_global_device_ids=true, to_apply=%region_2.0 | all-reduce | flops 1024 | bytes 8192 | tf_op jit(solution)/shard_map/pmax | solution.py:200
  152.0 0.0 copy-done.2
  (1 shorter events, 0.0 us)
Async XLA Ops:
  8.5 19.4 %copy-start.3 = (f32[3,512]{1,0:T(4,128)S(1)}, f32[3,512]{1,0:T(4,128)}, u32[]{:S(2)}) copy-start(f32[3,512]{1,0:T(4,128)} %param.5) | copy-start | bytes 18436
  8.5 56.7 %all-to-all-start = ((bf16[128,48,128]{2,1,0:T(8,128)(2,1)}), bf16[128,48,128]{2,1,0:T(8,128)(2,1)S(1)}, u32[]{:S(2)}, u32[]{:S(2)}) async-start(bf16[128,48,128]{2,1,0:T(8,128)(2,1)} %split_block.1), calls=%async_computation | async-start | bytes 3145728 | tf_op jit(solution)/shard_map/all_to_all | solution.py:194
  27.9 1.2 copy-start.1
  65.1 1.2 copy-start
  142.4 9.6 %copy-start.2 = (f32[32,1024]{1,0:T(8,128)}, f32[32,1024]{1,0:T(8,128)S(1)}, u32[]{:S(2)}) copy-start(f32[32,1024]{1,0:T(8,128)S(1)} %reduce_sum.9) | copy-start | bytes 393220

commit v2 on v1

v2 whole, which is shorter than its diff:
```python
import jax
import jax.numpy as jnp
from jax import lax
from jax.experimental import pallas as pl
from jax.experimental.pallas import tpu as pltpu
from jax.sharding import PartitionSpec as P

TLEN = 128
STEPS = 2
TPL = 16
CH = 384
TIME_DEV = 1024
LANES = 128

HI = 4
CUBES = 16
CLASSES = 8
STATION = 3
CLASS_CH = CUBES * STATION
SHIFTS = TLEN // 16
RUN_ROWS = 33
RUN = RUN_ROWS * LANES
PIECE = TPL * CH // LANES
SAMPLE_ROWS = 112
SEND_ROWS = STEPS * PIECE + SAMPLE_ROWS
VMEM = pltpu.CompilerParams(vmem_limit_bytes=56 * 1024 * 1024)


def cube_of(group):
    return (group // 32) * HI + (group // 4) % HI


def class_of(group):
    return ((group // 16) % 2) * 4 + group % 4


def group_index(cube, klass):
    z_hi, y_hi = divmod(cube, HI)
    z_lo, low = divmod(klass, 4)
    return z_hi * 32 + z_lo * 16 + y_hi * 4 + low


CLASS_GROUPS = [[group_index(cube, klass) for cube in range(CUBES)] for klass in range(CLASSES)]
CUBE_GROUPS = [[group_index(cube, klass) for klass in range(CLASSES)] for cube in range(CUBES)]


def iota(shape, axis):
    return lax.broadcasted_iota(jnp.int32, shape, axis)


def matmul(left, right):
    return jnp.dot(left, right, preferred_element_type=jnp.float32)


def one_hot(flags):
    return jnp.where(flags, 1.0, 0.0).astype(jnp.bfloat16)


def split_kernel(block_ref, out_ref, moved_ref):
    channel = iota((CH, 1), 0)
    station = channel // STATION
    column = (channel % STATION) * CUBES + cube_of(station)
    klass = class_of(station)
    for shift in range(SHIFTS):
        rows = block_ref[:, shift * 16 : shift * 16 + 16, :].reshape(TPL * 16, CH)
        target = ((klass + shift) % CLASSES) * CLASS_CH + column
        moved_ref[shift] = matmul(rows, one_hot(iota((CH, CH), 1) == target)).astype(jnp.bfloat16)
    for klass in range(CLASSES):
        for tile in range(CH // LANES):
            lanes = slice(tile * LANES, (tile + 1) * LANES)
            slot_of_lane = (iota((1, LANES), 1) + tile * LANES) // CLASS_CH
            slots = range(tile * LANES // CLASS_CH, (tile * LANES + LANES - 1) // CLASS_CH + 1)
            packed = moved_ref[(slots[0] - klass) % CLASSES, :, lanes]
            for slot in slots[1:]:
                packed = jnp.where(slot_of_lane == slot, moved_ref[(slot - klass) % CLASSES, :, lanes], packed)
            for template in range(TPL):
                at = template * PIECE + tile * 16
                out_ref[klass, at : at + 16, :] = packed[template * 16 : template * 16 + 16]


def split_block(block):
    return pl.pallas_call(
        split_kernel,
        out_shape=jax.ShapeDtypeStruct((CLASSES, TPL * PIECE, LANES), jnp.bfloat16),
        in_specs=[pl.BlockSpec(memory_space=pltpu.VMEM)],
        out_specs=pl.BlockSpec(memory_space=pltpu.VMEM),
        scratch_shapes=[pltpu.VMEM((SHIFTS, TPL * 16, CH), jnp.bfloat16)],
        compiler_params=VMEM,
        cost_estimate=pl.CostEstimate(flops=1_000_000_000, bytes_accessed=3 << 20, transcendentals=0),
        name="split_block",
    )(block)


def pack_kernel(place_ref, first_ref, second_ref, samples_ref, out_ref, wide_ref, stage_ref):
    run = place_ref[0]
    wide_ref[:, 0:1024, :] = samples_ref[...].astype(jnp.float32)
    wide_ref[:, 1024:, :] = jnp.zeros((STATION, 8, LANES), jnp.float32)
    stage_ref[STATION * RUN_ROWS :, :] = jnp.zeros((SAMPLE_ROWS - STATION * RUN_ROWS, LANES), jnp.float32)
    for cube in range(CUBES):
        z_hi, y_hi = divmod(cube, HI)
        out_ref[cube, 0:PIECE, :] = first_ref[cube * PIECE : (cube + 1) * PIECE, :]
        out_ref[cube, PIECE : 2 * PIECE, :] = second_ref[cube * PIECE : (cube + 1) * PIECE, :]
        start = pl.multiple_of(run * 128 + (z_hi * 256 + y_hi * 32), 32)
        for ch in range(STATION):
            stage_ref[ch * RUN_ROWS : (ch + 1) * RUN_ROWS, :] = wide_ref[ch, pl.ds(start, RUN_ROWS), :]
        out_ref[cube, 2 * PIECE :, :] = stage_ref[...].astype(jnp.bfloat16)


def pack(place, first, second, samples):
    return pl.pallas_call(
        pack_kernel,
        out_shape=jax.ShapeDtypeStruct((CUBES, SEND_ROWS, LANES), jnp.bfloat16),
        in_specs=[pl.BlockSpec(memory_space=pltpu.SMEM)] + [pl.BlockSpec(memory_space=pltpu.VMEM)] * 3,
        out_specs=pl.BlockSpec(memory_space=pltpu.VMEM),
        scratch_shapes=[
            pltpu.VMEM((STATION, 1032, LANES), jnp.float32),
            pltpu.VMEM((SAMPLE_ROWS, LANES), jnp.float32),
        ],
        compiler_params=VMEM,
        cost_estimate=pl.CostEstimate(flops=1_000_000, bytes_accessed=2 << 20, transcendentals=0),
        name="pack",
    )(place, first, second, samples)


def line_up_kernel(received_ref, out_ref, stage_ref):
    for cube in range(CUBES):
        stage_ref[cube * SAMPLE_ROWS : (cube + 1) * SAMPLE_ROWS, :] = received_ref[cube, 2 * PIECE :, :].astype(jnp.float32)
    for ch in range(STATION):
        for block in range(RUN_ROWS):
            rows = stage_ref[pl.ds(ch * RUN_ROWS + block, CUBES, stride=SAMPLE_ROWS), :]
            out_ref[ch * CUBES : (ch + 1) * CUBES, block * LANES : (block + 1) * LANES] = rows.astype(jnp.bfloat16)


def line_up(received):
    return pl.pallas_call(
        line_up_kernel,
        out_shape=jax.ShapeDtypeStruct((CLASS_CH, RUN), jnp.bfloat16),
        in_specs=[pl.BlockSpec(memory_space=pltpu.VMEM)],
        out_specs=pl.BlockSpec(memory_space=pltpu.VMEM),
        scratch_shapes=[pltpu.VMEM((CUBES * SAMPLE_ROWS, LANES), jnp.float32)],
        compiler_params=VMEM,
        cost_estimate=pl.CostEstimate(flops=1_000_000, bytes_accessed=1 << 20, transcendentals=0),
        name="line_up",
    )(received)


def correlate_kernel(place_ref, own_ref, other_ref, pieces_ref, out_ref, natural_ref, weight_ref, x_ref, product_ref):
    own_run, klass = place_ref[0], place_ref[1]
    for template in range(TPL):
        for step in range(STEPS):
            row = (template * STEPS + step) * 16
            for tile in range(CH // LANES):
                at = step * PIECE + tile * 16
                natural_ref[row : row + 16, tile * LANES : (tile + 1) * LANES] = pieces_ref[template, at : at + 16, :]
    rows = TPL * STEPS * 16
    wanted = iota((rows, 1), 0)
    lag, step, template = wanted // 32, (wanted // 16) % 2, wanted % 16
    order = one_hot(iota((rows, rows), 1) == (template * 2 + step) * 16 + lag)
    weight_ref[...] = matmul(order, natural_ref[...]).astype(jnp.bfloat16)
    for run, line_ref in enumerate((own_ref, other_ref)):
        line = line_ref[...].astype(jnp.float32)
        for shift in range(SHIFTS):
            moved = line if shift == 0 else pltpu.roll(line, RUN - 16 * shift, 1)
            at = pl.multiple_of(((klass + shift) % CLASSES) * CLASS_CH, 16)
            x_ref[pl.ds(at, CLASS_CH), :] = moved.astype(jnp.bfloat16)
        for start in range(0, RUN, 1408):
            product_ref[:, start : start + 1408] = matmul(weight_ref[...], x_ref[:, start : start + 1408])
        first = (own_run if run == 0 else 1 - own_run) * 4
        for part in range(4):
            total = product_ref[0:32, part * TIME_DEV : (part + 1) * TIME_DEV]
            for lag in range(1, 16):
                window = product_ref[lag * 32 : (lag + 1) * 32, part * TIME_DEV : (part + 1) * TIME_DEV + LANES]
                total = total + pltpu.roll(window, TIME_DEV + LANES - lag, 1)[:, :TIME_DEV]
            out_ref[first + part] = total


def correlate(place, own, other, pieces):
    return pl.pallas_call(
        correlate_kernel,
        out_shape=jax.ShapeDtypeStruct((CLASSES, STEPS * TPL, TIME_DEV), jnp.float32),
        in_specs=[pl.BlockSpec(memory_space=pltpu.SMEM)] + [pl.BlockSpec(memory_space=pltpu.VMEM)] * 3,
        out_specs=pl.BlockSpec(memory_space=pltpu.VMEM),
        scratch_shapes=[
            pltpu.VMEM((TPL * STEPS * 16, CH), jnp.bfloat16),
            pltpu.VMEM((TPL * STEPS * 16, CH), jnp.bfloat16),
            pltpu.VMEM((CH, RUN), jnp.bfloat16),
            pltpu.VMEM((TPL * STEPS * 16, RUN), jnp.float32),
        ],
        compiler_params=VMEM,
        cost_estimate=pl.CostEstimate(flops=3_400_000_000, bytes_accessed=3 << 20, transcendentals=0),
        name="correlate",
    )(place, own, other, pieces)


def exchange(array, groups):
    return lax.all_to_all(array, "group", 0, 0, axis_index_groups=groups, tiled=True)


def body(traces, scales, templates, owners):
    station_ch, samples_all = traces.shape
    place = jnp.stack([lax.axis_index("bank") % 2, class_of(lax.axis_index("group"))]).astype(jnp.int32)
    blocked = traces.astype(jnp.float32).reshape(station_ch, scales.shape[1], -1)
    samples = (blocked * scales[:, :, None]).astype(jnp.bfloat16).reshape(station_ch, samples_all // LANES, LANES)
    by_class = exchange(split_block(templates[0, 0]), CUBE_GROUPS)
    near = [lax.dynamic_index_in_dim(by_class, class_of(owners[step, 0]), 0, keepdims=False) for step in range(STEPS)]
    received = exchange(pack(place, near[0], near[1], samples), CLASS_GROUPS)
    own = line_up(received)
    other = lax.ppermute(own, "bank", [(0, 1), (1, 0), (2, 3), (3, 2)])
    far = [
        lax.dynamic_slice(received, (cube_of(owners[step, 0]), step * PIECE, 0), (1, PIECE, LANES))
        for step in range(STEPS)
    ]
    piece = jnp.concatenate(far, axis=1)
    pieces = exchange(jnp.broadcast_to(piece, (CUBES, STEPS * PIECE, LANES)), CLASS_GROUPS)
    partial = exchange(correlate(place, own, other, pieces), CUBE_GROUPS)
    scores = jnp.sum(partial, axis=0).reshape(STEPS, 1, TPL, TIME_DEV)
    best_score = lax.pmax(jnp.max(scores, axis=(0, 1, 2)), "bank")
    return (scores, best_score)


def solution(mesh):
    placed = (
        P("group", None),
        P("group", None),
        P("bank", "group", None, None, None),
        P(None, "bank"),
    )
    return jax.shard_map(
        body,
        mesh=mesh,
        in_specs=placed,
        out_specs=(P(None, "bank", None, "group"), P("group")),
        check_vma=False,
    )
```

time: 153 us -> 139 us (0.908)
  blocking collectives: 72 us -> 30 us
  starting transfers between devices: 19.4 us -> 37 us
  between operations: 0.69 us -> 6.18 us
  waiting for transfers between devices: 34.4 us -> 39.4 us
    all_to_all x2 -> x1, blocking collectives: 62.5 us -> 20.3 us  [exchange(): lax.all_to_all(array, 'group', 0, 0, axis_index_groups=groups, tiled=True)]
    all_to_all x1 -> x3, starting transfers between devices: 19.4 us -> 34.1 us  [exchange(): lax.all_to_all(array, 'group', 0, 0, axis_index_groups=groups, tiled=True)]
    all_to_all x1 -> x3, waiting for transfers between devices: 34.4 us -> 38 us  [exchange(): lax.all_to_all(array, 'group', 0, 0, axis_index_groups=groups, tiled=True)]
    ppermute x0 -> x1, starting transfers between devices: none -> 2.88 us  [body(): other = lax.ppermute(own, 'bank', [(0, 1), (1, 0), (2, 3), (3, 2)])]
    pallas_call x2 -> x3, Pallas kernels: 11.1 us -> 9.73 us  [the longest x1 4.99 us: split_block(): pl.pallas_call(split_kernel, out_shape=jax.ShapeDtypeStruct((CLASSES, TPL...]
  transfers between devices with their start and end apart: 1 -> 4, of which waited for: 1 -> 4; matrix products, arithmetic and copies ran while one was open for 2% -> 3% of each run, Pallas kernels for 0% -> 2%
where the time goes in v2:
time: 139 us
  waiting for transfers between devices  39.4 us (28%)
  starting transfers between devices  37 us (27%)
  blocking collectives  30 us (22%)
  Pallas kernels  20 us (14%)
  between operations  6.18 us (4%)
  local copies, waits for them, and re-layouts  3.77 us (3%)
  other arithmetic  2.34 us (2%)
    all_to_all x3, waiting for transfers between devices, exchange(): lax.all_to_all(array, 'group', 0, 0, axis_index_groups=groups, tiled=True)  38 us
    all_to_all x3, starting transfers between devices, exchange(): lax.all_to_all(array, 'group', 0, 0, axis_index_groups=groups, tiled=True)  34.1 us
    all_to_all x1, blocking collectives, exchange(): lax.all_to_all(array, 'group', 0, 0, axis_index_groups=groups, tiled=True)  20.3 us
    pallas_call x1, Pallas kernels, correlate(): pl.pallas_call(correlate_kernel, out_shape=jax.ShapeDtypeStruct((CLASSES,...  10.2 us
    pmax x1, blocking collectives, body(): best_score = lax.pmax(jnp.max(scores, axis=(0, 1, 2)), 'bank')  9.65 us
    pallas_call x1, Pallas kernels, split_block(): pl.pallas_call(split_kernel, out_shape=jax.ShapeDtypeStruct((CLASSES, TPL...  4.99 us
    ppermute x1, starting transfers between devices, body(): other = lax.ppermute(own, 'bank', [(0, 1), (1, 0), (2, 3), (3, 2)])  2.88 us
  transfers between devices with their start and end apart: 4, of which 4 were waited for; matrix products, arithmetic and copies ran while one was open for 3% of the time, Pallas kernels for 2%

profile of v2, /device:TPU:1, one launch (start us, length us, event | category | flops | bytes accessed | tf_op | source)
XLA Modules:
  0.0 138.7 jit_solution(452316075482832648)
XLA Ops:
  0.6 5.0 %split_block.1 = bf16[8,768,128]{2,1,0:T(8,128)(2,1)} custom-call(bf16[16,128,384]{2,1,0:T(8,128)(2,1)} %bitcast.19), custom_call_target="tpu_custom_call" | custom-call | flops 1000000000 | bytes 3145728 | tf_op jit(solution)/shard_map/split_block/pallas_call | solution.py:82
  5.6 6.3 %all-to-all-start = ((bf16[8,768,128]{2,1,0:T(8,128)(2,1)}), bf16[8,768,128]{2,1,0:T(8,128)(2,1)S(1)}, u32[]{:S(2)}, u32[]{:S(2)}) async-start(bf16[8,768,128]{2,1,0:T(8,128)(2,1)} %split_block.1), calls=%async_computation | async-start | bytes 3145728 | tf_op jit(solution)/shard_map/all_to_all | solution.py:196
  11.9 0.6 fusion.1
  17.8 0.3 mul.31
  18.1 0.5 mul.32
  18.6 0.7 pad_add_fusion.place_ref
  19.2 0.2 convert_bitcast_fusion
  19.5 1.4 fusion.samples_ref
  20.8 9.0 %all-to-all-done = bf16[8,768,128]{2,1,0:T(8,128)(2,1)S(1)} async-done(((bf16[8,768,128]{2,1,0:T(8,128)(2,1)}), bf16[8,768,128]{2,1,0:T(8,128)(2,1)S(1)}, u32[]{:S(2)}, u32[]{:S(2)}) %all-to-all-start) | async-done | bytes 1572896 | tf_op jit(solution)/shard_map/all_to_all | solution.py:196
  29.8 0.8 dynamic-slice_bitcast_fusion
  30.6 2.5 %pack.1 = bf16[16,208,128]{2,1,0:T(8,128)(2,1)} custom-call(s32[2]{0:T(128)} %pad_add_fusion.place_ref, bf16[768,128]{1,0:T(8,128)(2,1)} %get-tuple-element.3.first_ref, bf16[768,128]{1,0:T(8,128)(2,1)} %get-tuple-element.2.second_ref, bf16[3,1024,128]{2,1,0:T(8,128)(2,1)} %fusion.samples_ref), custom_call_target="tpu_custom_call" | custom-call | flops 1000000 | bytes 2097152 | tf_op jit(solution)/shard_map/pack/pallas_call | solution.py:110
  33.1 17.8 %all-to-all-start.1 = ((bf16[16,208,128]{2,1,0:T(8,128)(2,1)}), bf16[16,208,128]{2,1,0:T(8,128)(2,1)S(1)}, u32[]{:S(2)}, u32[]{:S(2)}) async-start(bf16[16,208,128]{2,1,0:T(8,128)(2,1)} %pack.1), calls=%async_computation.1 | async-start | bytes 1703936 | tf_op jit(solution)/shard_map/all_to_all | solution.py:196
  51.0 21.0 %all-to-all-done.1.received_ref = bf16[16,208,128]{2,1,0:T(8,128)(2,1)S(1)} async-done(((bf16[16,208,128]{2,1,0:T(8,128)(2,1)}), bf16[16,208,128]{2,1,0:T(8,128)(2,1)S(1)}, u32[]{:S(2)}, u32[]{:S(2)}) %all-to-all-start.1) | async-done | bytes 852000 | tf_op jit(solution)/shard_map/all_to_all | solution.py:196
  72.0 0.9 broadcast_in_dim.9
  72.9 10.1 %all-to-all-start.2 = ((bf16[16,96,128]{2,1,0:T(8,128)(2,1)}), bf16[16,96,128]{2,1,0:T(8,128)(2,1)S(1)}, u32[]{:S(2)}, u32[]{:S(2)}) async-start(bf16[16,96,128]{2,1,0:T(8,128)(2,1)} %broadcast_in_dim.9), calls=%async_computation.2 | async-start | bytes 786432 | tf_op jit(solution)/shard_map/all_to_all | solution.py:196
  83.0 2.2 %line_up.1.own_ref = bf16[48,4224]{1,0:T(8,128)(2,1)} custom-call(bf16[16,208,128]{2,1,0:T(8,128)(2,1)} %copy-done), custom_call_target="tpu_custom_call" | custom-call | flops 1000000 | bytes 1048576 | tf_op jit(solution)/shard_map/line_up/pallas_call | solution.py:135
  85.2 2.9 %collective-permute-start = (bf16[48,4224]{1,0:T(8,128)(2,1)}, bf16[48,4224]{1,0:T(8,128)(2,1)S(1)}, u32[]{:S(2)}, u32[]{:S(2)}) collective-permute-start(bf16[48,4224]{1,0:T(8,128)(2,1)} %line_up.1.own_ref), channel_id=1, source_target_pairs={{0,1},{1,0},{2,3},{3,2},{4,5},{5,4},{6,7},{7,6},{8,9},{9,8},{10,11... | collective-permute-start | bytes 1216520 | tf_op jit(solution)/shard_map/ppermute | solution.py:208
  88.1 1.4 collective-permute-done.other_ref
  89.5 8.0 %all-to-all-done.2.pieces_ref = bf16[16,96,128]{2,1,0:T(8,128)(2,1)S(1)} async-done(((bf16[16,96,128]{2,1,0:T(8,128)(2,1)}), bf16[16,96,128]{2,1,0:T(8,128)(2,1)S(1)}, u32[]{:S(2)}, u32[]{:S(2)}) %all-to-all-start.2) | async-done | bytes 393248 | tf_op jit(solution)/shard_map/all_to_all | solution.py:196
  97.6 0.8 copy-done.3
  98.3 10.2 %correlate.1 = f32[8,32,1024]{2,1,0:T(8,128)} custom-call(s32[2]{0:T(128)} %pad_add_fusion.place_ref, bf16[48,4224]{1,0:T(8,128)(2,1)} %line_up.1.own_ref, bf16[48,4224]{1,0:T(8,128)(2,1)} %copy-done.6, bf16[16,96,128]{2,1,0:T(8,128)(2,1)} %copy-done.3), custom_call_target="tpu_custom_call" | custom-call | flops 3400000000 | bytes 3145728 | tf_op jit(solution)/shard_map/correlate/pallas_call | solution.py:178
  108.6 20.3 %all_to_all.20 = f32[8,32,1024]{2,1,0:T(8,128)S(1)} all-to-all(f32[8,32,1024]{2,1,0:T(8,128)} %correlate.1), channel_id=1, replica_groups={{0,4,8,12,64,68,72,76},{16,20,24,28,80,84,88,92},{32,36,40,44,96,100,10..., dimensions={0} | all-to-all | bytes 2097152 | tf_op jit(solution)/shard_map/all_to_all | solution.py:196
  128.9 0.1 reduce_sum.9
  129.0 9.6 %pmax.7 = f32[1024]{0:T(1024)} all-reduce(f32[1024]{0:T(1024)S(1)} %reduce_max.9), channel_id=1, replica_groups=mesh['group'=128,'bank'=4] {'bank'}, use_global_device_ids=true, to_apply=%region_2.3 | all-reduce | flops 1024 | bytes 8192 | tf_op jit(solution)/shard_map/pmax | solution.py:217
  (16 shorter events, 0.1 us)
Async XLA Ops:
  5.6 6.3 %copy-start.5 = (s32[2,1]{0,1:T(1,128)S(1)}, s32[2,1]{0,1:T(1,128)}, u32[]{:S(2)}) copy-start(s32[2,1]{0,1:T(1,128)} %param.7) | copy-start | bytes 28
  5.6 12.2 %copy-start.4 = (f32[3,512]{1,0:T(4,128)S(1)}, f32[3,512]{1,0:T(4,128)}, u32[]{:S(2)}) copy-start(f32[3,512]{1,0:T(4,128)} %param.5) | copy-start | bytes 18436
  5.6 24.2 %all-to-all-start = ((bf16[8,768,128]{2,1,0:T(8,128)(2,1)}), bf16[8,768,128]{2,1,0:T(8,128)(2,1)S(1)}, u32[]{:S(2)}, u32[]{:S(2)}) async-start(bf16[8,768,128]{2,1,0:T(8,128)(2,1)} %split_block.1), calls=%async_computation | async-start | bytes 3145728 | tf_op jit(solution)/shard_map/all_to_all | solution.py:196
  11.9 7.4 %copy-start.1 = (bf16[3,131072]{1,0:T(4,128)(2,1)S(1)}, bf16[3,131072]{1,0:T(4,128)(2,1)}, u32[]{:S(2)}) copy-start(bf16[3,131072]{1,0:T(4,128)(2,1)} %param.4) | copy-start | bytes 2359300
  33.1 38.9 %all-to-all-start.1 = ((bf16[16,208,128]{2,1,0:T(8,128)(2,1)}), bf16[16,208,128]{2,1,0:T(8,128)(2,1)S(1)}, u32[]{:S(2)}, u32[]{:S(2)}) async-start(bf16[16,208,128]{2,1,0:T(8,128)(2,1)} %pack.1), calls=%async_computation.1 | async-start | bytes 1703936 | tf_op jit(solution)/shard_map/all_to_all | solution.py:196
  72.0 11.0 %copy-start = (bf16[16,208,128]{2,1,0:T(8,128)(2,1)}, bf16[16,208,128]{2,1,0:T(8,128)(2,1)S(1)}, u32[]{:S(2)}) copy-start(bf16[16,208,128]{2,1,0:T(8,128)(2,1)S(1)} %all-to-all-done.1.received_ref) | copy-start | bytes 2555908
  72.9 24.7 %all-to-all-start.2 = ((bf16[16,96,128]{2,1,0:T(8,128)(2,1)}), bf16[16,96,128]{2,1,0:T(8,128)(2,1)S(1)}, u32[]{:S(2)}, u32[]{:S(2)}) async-start(bf16[16,96,128]{2,1,0:T(8,128)(2,1)} %broadcast_in_dim.9), calls=%async_computation.2 | async-start | bytes 786432 | tf_op jit(solution)/shard_map/all_to_all | solution.py:196
  85.2 4.3 %collective-permute-start = (bf16[48,4224]{1,0:T(8,128)(2,1)}, bf16[48,4224]{1,0:T(8,128)(2,1)S(1)}, u32[]{:S(2)}, u32[]{:S(2)}) collective-permute-start(bf16[48,4224]{1,0:T(8,128)(2,1)} %line_up.1.own_ref), channel_id=1, source_target_pairs={{0,1},{1,0},{2,3},{3,2},{4,5},{5,4},{6,7},{7,6},{8,9},{9,8},{10,11... | collective-permute-start | bytes 1216520 | tf_op jit(solution)/shard_map/ppermute | solution.py:208
  89.5 8.0 %copy-start.6 = (bf16[48,4224]{1,0:T(8,128)(2,1)}, bf16[48,4224]{1,0:T(8,128)(2,1)S(1)}, u32[]{:S(2)}) copy-start(bf16[48,4224]{1,0:T(8,128)(2,1)S(1)} %collective-permute-done.other_ref) | copy-start | bytes 1216516
  97.6 0.8 copy-start.3
  129.0 9.7 %copy-start.2 = (f32[32,1024]{1,0:T(8,128)}, f32[32,1024]{1,0:T(8,128)S(1)}, u32[]{:S(2)}) copy-start(f32[32,1024]{1,0:T(8,128)S(1)} %reduce_sum.9) | copy-start | bytes 393220

commit v3 on v2

--- a/solution.py
+++ b/solution.py
@@ -23,7 +23,14 @@
 PIECE = TPL * CH // LANES
 SAMPLE_ROWS = 112
 SEND_ROWS = STEPS * PIECE + SAMPLE_ROWS
-VMEM = pltpu.CompilerParams(vmem_limit_bytes=56 * 1024 * 1024)
+CHUNKS = ((0, 1152), (1152, 2176), (2176, 3200), (3200, RUN))
+LAGS = 8
+DEPTH = TLEN // LAGS * CLASS_CH
+ROWS = LAGS * STEPS * TPL
+
+
+def vmem(mebibytes):
+    return pltpu.CompilerParams(vmem_limit_bytes=mebibytes * 1024 * 1024)
 
 
 def cube_of(group):
@@ -56,7 +63,7 @@
     return jnp.where(flags, 1.0, 0.0).astype(jnp.bfloat16)
 
 
-def split_kernel(block_ref, out_ref, moved_ref):
+def split_kernel(block_ref, out_ref, moved_ref, packed_ref, sems):
     channel = iota((CH, 1), 0)
     station = channel // STATION
     column = (channel % STATION) * CUBES + cube_of(station)
@@ -65,6 +72,7 @@
         rows = block_ref[:, shift * 16 : shift * 16 + 16, :].reshape(TPL * 16, CH)
         target = ((klass + shift) % CLASSES) * CLASS_CH + column
         moved_ref[shift] = matmul(rows, one_hot(iota((CH, CH), 1) == target)).astype(jnp.bfloat16)
+    copies = []
     for klass in range(CLASSES):
         for tile in range(CH // LANES):
             lanes = slice(tile * LANES, (tile + 1) * LANES)
@@ -75,17 +83,25 @@
                 packed = jnp.where(slot_of_lane == slot, moved_ref[(slot - klass) % CLASSES, :, lanes], packed)
             for template in range(TPL):
                 at = template * PIECE + tile * 16
-                out_ref[klass, at : at + 16, :] = packed[template * 16 : template * 16 + 16]
+                packed_ref[klass, at : at + 16, :] = packed[template * 16 : template * 16 + 16]
+        copies.append(pltpu.make_async_copy(packed_ref.at[klass], out_ref.at[klass], sems.at[klass]))
+        copies[-1].start()
+    for copy in copies:
+        copy.wait()
 
 
 def split_block(block):
     return pl.pallas_call(
         split_kernel,
-        out_shape=jax.ShapeDtypeStruct((CLASSES, TPL * PIECE, LANES), jnp.bfloat16),
+        out_shape=pltpu.HBM((CLASSES, TPL * PIECE, LANES), jnp.bfloat16),
         in_specs=[pl.BlockSpec(memory_space=pltpu.VMEM)],
-        out_specs=pl.BlockSpec(memory_space=pltpu.VMEM),
-        scratch_shapes=[pltpu.VMEM((SHIFTS, TPL * 16, CH), jnp.bfloat16)],
-        compiler_params=VMEM,
+        out_specs=pl.BlockSpec(memory_space=pl.ANY),
+        scratch_shapes=[
+            pltpu.VMEM((SHIFTS, TPL * 16, CH), jnp.bfloat16),
+            pltpu.VMEM((CLASSES, TPL * PIECE, LANES), jnp.bfloat16),
+            pltpu.SemaphoreType.DMA((CLASSES,)),
+        ],
+        compiler_params=vmem(12),
         cost_estimate=pl.CostEstimate(flops=1_000_000_000, bytes_accessed=3 << 20, transcendentals=0),
         name="split_block",
     )(block)
@@ -116,7 +132,7 @@
             pltpu.VMEM((STATION, 1032, LANES), jnp.float32),
             pltpu.VMEM((SAMPLE_ROWS, LANES), jnp.float32),
         ],
-        compiler_params=VMEM,
+        compiler_params=vmem(8),
         cost_estimate=pl.CostEstimate(flops=1_000_000, bytes_accessed=2 << 20, transcendentals=0),
         name="pack",
     )(place, first, second, samples)
@@ -138,58 +154,63 @@
         in_specs=[pl.BlockSpec(memory_space=pltpu.VMEM)],
         out_specs=pl.BlockSpec(memory_space=pltpu.VMEM),
         scratch_shapes=[pltpu.VMEM((CUBES * SAMPLE_ROWS, LANES), jnp.float32)],
-        compiler_params=VMEM,
+        compiler_params=vmem(8),
         cost_estimate=pl.CostEstimate(flops=1_000_000, bytes_accessed=1 << 20, transcendentals=0),
         name="line_up",
     )(received)
 
 
-def correlate_kernel(place_ref, own_ref, other_ref, pieces_ref, out_ref, natural_ref, weight_ref, x_ref, product_ref):
+def correlate_kernel(
+    place_ref, pieces_ref, own_ref, other_ref, out_ref, natural_ref, weight_ref, moved_ref, product_ref
+):
     own_run, klass = place_ref[0], place_ref[1]
+    for run, line_ref in enumerate((own_ref, other_ref)):
+        line = line_ref[...]
+        for odd in range(2):
+            for shift in range(SHIFTS):
+                by = 16 * shift + 8 * odd
+                at = odd * CH + shift * CLASS_CH
+                moved_ref[run, at : at + CLASS_CH, :] = pltpu.roll(line, RUN - by, 1) if by else line
     for template in range(TPL):
         for step in range(STEPS):
             row = (template * STEPS + step) * 16
             for tile in range(CH // LANES):
                 at = step * PIECE + tile * 16
                 natural_ref[row : row + 16, tile * LANES : (tile + 1) * LANES] = pieces_ref[template, at : at + 16, :]
-    rows = TPL * STEPS * 16
-    wanted = iota((rows, 1), 0)
+    wanted = iota((2 * ROWS, 1), 0)
     lag, step, template = wanted // 32, (wanted // 16) % 2, wanted % 16
-    order = one_hot(iota((rows, rows), 1) == (template * 2 + step) * 16 + lag)
-    weight_ref[...] = matmul(order, natural_ref[...]).astype(jnp.bfloat16)
-    for run, line_ref in enumerate((own_ref, other_ref)):
-        line = line_ref[...].astype(jnp.float32)
-        for shift in range(SHIFTS):
-            moved = line if shift == 0 else pltpu.roll(line, RUN - 16 * shift, 1)
-            at = pl.multiple_of(((klass + shift) % CLASSES) * CLASS_CH, 16)
-            x_ref[pl.ds(at, CLASS_CH), :] = moved.astype(jnp.bfloat16)
-        for start in range(0, RUN, 1408):
-            product_ref[:, start : start + 1408] = matmul(weight_ref[...], x_ref[:, start : start + 1408])
+    order = one_hot(iota((2 * ROWS, 2 * ROWS), 1) == (template * 2 + step) * 16 + lag)
+    ordered = pltpu.roll(matmul(order, natural_ref[...]), (CH - klass * CLASS_CH) % CH, 1).astype(jnp.bfloat16)
+    weight_ref[:, 0:CH] = ordered[0:ROWS]
+    weight_ref[:, CH:] = ordered[ROWS:]
+    for run in range(2):
         first = (own_run if run == 0 else 1 - own_run) * 4
-        for part in range(4):
-            total = product_ref[0:32, part * TIME_DEV : (part + 1) * TIME_DEV]
-            for lag in range(1, 16):
-                window = product_ref[lag * 32 : (lag + 1) * 32, part * TIME_DEV : (part + 1) * TIME_DEV + LANES]
+        for part, (start, stop) in enumerate(CHUNKS):
+            product_ref[run, :, start:stop] = matmul(weight_ref[...], moved_ref[run, :, start:stop])
+            at = part * TIME_DEV
+            total = product_ref[run, 0:32, at : at + TIME_DEV]
+            for lag in range(1, LAGS):
+                window = product_ref[run, lag * 32 : (lag + 1) * 32, at : at + TIME_DEV + LANES]
                 total = total + pltpu.roll(window, TIME_DEV + LANES - lag, 1)[:, :TIME_DEV]
             out_ref[first + part] = total
 
 
-def correlate(place, own, other, pieces):
+def correlate(place, pieces, own, other):
     return pl.pallas_call(
         correlate_kernel,
         out_shape=jax.ShapeDtypeStruct((CLASSES, STEPS * TPL, TIME_DEV), jnp.float32),
         in_specs=[pl.BlockSpec(memory_space=pltpu.SMEM)] + [pl.BlockSpec(memory_space=pltpu.VMEM)] * 3,
         out_specs=pl.BlockSpec(memory_space=pltpu.VMEM),
         scratch_shapes=[
-            pltpu.VMEM((TPL * STEPS * 16, CH), jnp.bfloat16),
-            pltpu.VMEM((TPL * STEPS * 16, CH), jnp.bfloat16),
-            pltpu.VMEM((CH, RUN), jnp.bfloat16),
-            pltpu.VMEM((TPL * STEPS * 16, RUN), jnp.float32),
+            pltpu.VMEM((2 * ROWS, CH), jnp.bfloat16),
+            pltpu.VMEM((ROWS, DEPTH), jnp.bfloat16),
+            pltpu.VMEM((2, DEPTH, RUN), jnp.bfloat16),
+            pltpu.VMEM((2, ROWS, RUN), jnp.float32),
         ],
-        compiler_params=VMEM,
+        compiler_params=vmem(32),
         cost_estimate=pl.CostEstimate(flops=3_400_000_000, bytes_accessed=3 << 20, transcendentals=0),
         name="correlate",
-    )(place, own, other, pieces)
+    )(place, pieces, own, other)
 
 
 def exchange(array, groups):
@@ -204,15 +225,15 @@
     by_class = exchange(split_block(templates[0, 0]), CUBE_GROUPS)
     near = [lax.dynamic_index_in_dim(by_class, class_of(owners[step, 0]), 0, keepdims=False) for step in range(STEPS)]
     received = exchange(pack(place, near[0], near[1], samples), CLASS_GROUPS)
-    own = line_up(received)
-    other = lax.ppermute(own, "bank", [(0, 1), (1, 0), (2, 3), (3, 2)])
     far = [
         lax.dynamic_slice(received, (cube_of(owners[step, 0]), step * PIECE, 0), (1, PIECE, LANES))
         for step in range(STEPS)
     ]
     piece = jnp.concatenate(far, axis=1)
     pieces = exchange(jnp.broadcast_to(piece, (CUBES, STEPS * PIECE, LANES)), CLASS_GROUPS)
-    partial = exchange(correlate(place, own, other, pieces), CUBE_GROUPS)
+    own = line_up(received)
+    other = lax.ppermute(own, "bank", [(0, 1), (1, 0), (2, 3), (3, 2)])
+    partial = exchange(correlate(place, pieces, own, other), CUBE_GROUPS)
     scores = jnp.sum(partial, axis=0).reshape(STEPS, 1, TPL, TIME_DEV)
     best_score = lax.pmax(jnp.max(scores, axis=(0, 1, 2)), "bank")
     return (scores, best_score)

time: 139 us -> 133 us (0.957)
  Pallas kernels: 20 us -> 12.2 us
  waiting for transfers between devices: 39.4 us -> 43 us
  other arithmetic: 2.34 us -> 0.86 us
    all_to_all x3, waiting for transfers between devices: 38 us -> 41.7 us  [exchange(): lax.all_to_all(array, 'group', 0, 0, axis_index_groups=groups, tiled=True)]
    pallas_call x1, Pallas kernels: 10.2 us -> 6.64 us  [correlate(): pl.pallas_call(correlate_kernel, out_shape=jax.ShapeDtypeStruct((CLASSES,...]
    pallas_call x1, Pallas kernels: 2.24 us -> 0.32 us  [line_up(): pl.pallas_call(line_up_kernel, out_shape=jax.ShapeDtypeStruct((CLASS_CH,...]
    pmax x1, blocking collectives: 9.65 us -> 11.4 us  [body(): best_score = lax.pmax(jnp.max(scores, axis=(0, 1, 2)), 'bank')]
    all_to_all x1, blocking collectives: 20.3 us -> 18.8 us  [exchange(): lax.all_to_all(array, 'group', 0, 0, axis_index_groups=groups, tiled=True)]
    pallas_call x1, Pallas kernels: 4.99 us -> 3.52 us  [split_block(): pl.pallas_call(split_kernel, out_shape=pltpu.HBM((CLASSES, TPL * PIECE, L...]
  transfers between devices with their start and end apart: 4 -> 4, of which waited for: 4 -> 4; matrix products, arithmetic and copies ran while one was open for 3% -> 2% of each run, Pallas kernels for 2% -> 0%
where the time goes in v3:
time: 133 us
  waiting for transfers between devices  43 us (32%)
  starting transfers between devices  36.7 us (28%)
  blocking collectives  30.2 us (23%)
  Pallas kernels  12.2 us (9%)
  between operations  6.22 us (5%)
  local copies, waits for them, and re-layouts  3.55 us (3%)
    all_to_all x3, waiting for transfers between devices, exchange(): lax.all_to_all(array, 'group', 0, 0, axis_index_groups=groups, tiled=True)  41.7 us
    all_to_all x3, starting transfers between devices, exchange(): lax.all_to_all(array, 'group', 0, 0, axis_index_groups=groups, tiled=True)  33.9 us
    all_to_all x1, blocking collectives, exchange(): lax.all_to_all(array, 'group', 0, 0, axis_index_groups=groups, tiled=True)  18.8 us
    pmax x1, blocking collectives, body(): best_score = lax.pmax(jnp.max(scores, axis=(0, 1, 2)), 'bank')  11.4 us
    pallas_call x1, Pallas kernels, correlate(): pl.pallas_call(correlate_kernel, out_shape=jax.ShapeDtypeStruct((CLASSES,...  6.64 us
    pallas_call x1, Pallas kernels, split_block(): pl.pallas_call(split_kernel, out_shape=pltpu.HBM((CLASSES, TPL * PIECE, L...  3.52 us
    ppermute x1, starting transfers between devices, body(): other = lax.ppermute(own, 'bank', [(0, 1), (1, 0), (2, 3), (3, 2)])  2.71 us
  transfers between devices with their start and end apart: 4, of which 4 were waited for; matrix products, arithmetic and copies ran while one was open for 2% of the time, Pallas kernels for 0%

profile of v3, /device:TPU:1, one launch (start us, length us, event | category | flops | bytes accessed | tf_op | source)
XLA Modules:
  0.0 132.7 jit_solution(8334795871829628886)
XLA Ops:
  0.6 1.4 %copy-done = bf16[1,1,16,128,384]{4,3,2,1,0:T(8,128)(2,1)S(1)} copy-done((bf16[1,1,16,128,384]{4,3,2,1,0:T(8,128)(2,1)S(1)}, bf16[1,1,16,128,384]{4,3,2,1,0:T(8,128)(2,1)}, u32[]{:S(2)}) %copy-start) | copy-done | bytes 1572888
  2.0 3.5 %split_block.1 = bf16[8,768,128]{2,1,0:T(8,128)(2,1)} custom-call(bf16[16,128,384]{2,1,0:T(8,128)(2,1)S(1)} %bitcast.18), custom_call_target="tpu_custom_call" | custom-call | flops 1000000000 | bytes 3145728 | tf_op jit(solution)/shard_map/split_block/pallas_call | solution.py:94
  5.6 0.0 copy-start.4
  5.6 6.2 %all-to-all-start = ((bf16[8,768,128]{2,1,0:T(8,128)(2,1)}), bf16[8,768,128]{2,1,0:T(8,128)(2,1)S(1)}, u32[]{:S(2)}, u32[]{:S(2)}) async-start(bf16[8,768,128]{2,1,0:T(8,128)(2,1)} %split_block.1), calls=%async_computation | async-start | bytes 3145728 | tf_op jit(solution)/shard_map/all_to_all | solution.py:217
  11.8 0.6 fusion.1
  17.7 0.3 mul.31
  17.9 0.5 mul.32
  18.4 0.1 pad_add_fusion.place_ref
  18.5 0.2 convert_bitcast_fusion
  18.7 0.5 fusion.samples_ref
  19.2 10.4 %all-to-all-done = bf16[8,768,128]{2,1,0:T(8,128)(2,1)S(1)} async-done(((bf16[8,768,128]{2,1,0:T(8,128)(2,1)}), bf16[8,768,128]{2,1,0:T(8,128)(2,1)S(1)}, u32[]{:S(2)}, u32[]{:S(2)}) %all-to-all-start) | async-done | bytes 1572896 | tf_op jit(solution)/shard_map/all_to_all | solution.py:217
  29.7 1.7 %pack.1 = bf16[16,208,128]{2,1,0:T(8,128)(2,1)} custom-call(s32[2]{0:T(128)S(1)} %pad_add_fusion.place_ref, bf16[768,128]{1,0:T(8,128)(2,1)S(1)} %get-tuple-element.3.first_ref, bf16[768,128]{1,0:T(8,128)(2,1)S(1)} %get-tuple-element.2.second_ref, bf16[3,1024,128]{2,1,0:T(8,128)(2,1)S(1)} %fusion.samples_ref), custom_call_target="tpu_custom_call" | custom-call | flops 1000000 | bytes 2097152 | tf_op jit(solution)/shard_map/pack/pallas_call | solution.py:126
  31.4 17.8 %all-to-all-start.1 = ((bf16[16,208,128]{2,1,0:T(8,128)(2,1)}), bf16[16,208,128]{2,1,0:T(8,128)(2,1)S(1)}, u32[]{:S(2)}, u32[]{:S(2)}) async-start(bf16[16,208,128]{2,1,0:T(8,128)(2,1)} %pack.1), calls=%async_computation.1 | async-start | bytes 1703936 | tf_op jit(solution)/shard_map/all_to_all | solution.py:217
  49.2 21.0 %all-to-all-done.1.received_ref = bf16[16,208,128]{2,1,0:T(8,128)(2,1)S(1)} async-done(((bf16[16,208,128]{2,1,0:T(8,128)(2,1)}), bf16[16,208,128]{2,1,0:T(8,128)(2,1)S(1)}, u32[]{:S(2)}, u32[]{:S(2)}) %all-to-all-start.1) | async-done | bytes 852000 | tf_op jit(solution)/shard_map/all_to_all | solution.py:217
  70.3 0.8 broadcast_in_dim.9
  71.1 10.0 %all-to-all-start.2 = ((bf16[16,96,128]{2,1,0:T(8,128)(2,1)}), bf16[16,96,128]{2,1,0:T(8,128)(2,1)S(1)}, u32[]{:S(2)}, u32[]{:S(2)}) async-start(bf16[16,96,128]{2,1,0:T(8,128)(2,1)} %broadcast_in_dim.9), calls=%async_computation.2 | async-start | bytes 786432 | tf_op jit(solution)/shard_map/all_to_all | solution.py:217
  81.1 0.3 line_up.1.own_ref
  81.4 2.7 %collective-permute-start = (bf16[48,4224]{1,0:T(8,128)(2,1)S(1)}, bf16[48,4224]{1,0:T(8,128)(2,1)S(1)}, u32[]{:S(2)}, u32[]{:S(2)}) collective-permute-start(bf16[48,4224]{1,0:T(8,128)(2,1)S(1)} %line_up.1.own_ref), channel_id=1, source_target_pairs={{0,1},{1,0},{2,3},{3,2},{4,5},{5,4},{6,7},{7,6},{8,9},{9,8},{10,11... | collective-permute-start | bytes 1216520 | tf_op jit(solution)/shard_map/ppermute | solution.py:235
  84.1 1.3 %collective-permute-done.other_ref = bf16[48,4224]{1,0:T(8,128)(2,1)S(1)} collective-permute-done((bf16[48,4224]{1,0:T(8,128)(2,1)S(1)}, bf16[48,4224]{1,0:T(8,128)(2,1)S(1)}, u32[]{:S(2)}, u32[]{:S(2)}) %collective-permute-start) | collective-permute-done | bytes 405536 | tf_op jit(solution)/shard_map/ppermute | solution.py:235
  85.5 10.2 %all-to-all-done.2.pieces_ref = bf16[16,96,128]{2,1,0:T(8,128)(2,1)S(1)} async-done(((bf16[16,96,128]{2,1,0:T(8,128)(2,1)}), bf16[16,96,128]{2,1,0:T(8,128)(2,1)S(1)}, u32[]{:S(2)}, u32[]{:S(2)}) %all-to-all-start.2) | async-done | bytes 393248 | tf_op jit(solution)/shard_map/all_to_all | solution.py:217
  95.7 6.6 %correlate.1 = f32[8,32,1024]{2,1,0:T(8,128)S(1)} custom-call(s32[2]{0:T(128)S(1)} %pad_add_fusion.place_ref, bf16[16,96,128]{2,1,0:T(8,128)(2,1)S(1)} %all-to-all-done.2.pieces_ref, bf16[48,4224]{1,0:T(8,128)(2,1)S(1)} %line_up.1.own_ref, bf16[48,4224]{1,0:T(8,128)(2,1)S(1)} %collective-permute-done.other_ref), custom_call_target="tpu_custom_call" | custom-call | flops 3400000000 | bytes 3145728 | tf_op jit(solution)/shard_map/correlate/pallas_call | solution.py:199
  102.3 18.8 %all_to_all.20 = f32[8,32,1024]{2,1,0:T(8,128)S(1)} all-to-all(f32[8,32,1024]{2,1,0:T(8,128)S(1)} %correlate.1), channel_id=1, replica_groups={{0,4,8,12,64,68,72,76},{16,20,24,28,80,84,88,92},{32,36,40,44,96,100,10..., dimensions={0} | all-to-all | bytes 2097152 | tf_op jit(solution)/shard_map/all_to_all | solution.py:217
  121.1 0.1 reduce_sum.9
  121.2 11.4 %pmax.7 = f32[1024]{0:T(1024)} all-reduce(f32[1024]{0:T(1024)S(1)} %reduce_max.9), channel_id=1, replica_groups=mesh['group'=128,'bank'=4] {'bank'}, use_global_device_ids=true, to_apply=%region_2.3 | all-reduce | flops 1024 | bytes 8192 | tf_op jit(solution)/shard_map/pmax | solution.py:238
  (12 shorter events, 0.1 us)
Async XLA Ops:
  0.6 1.4 %copy-start = (bf16[1,1,16,128,384]{4,3,2,1,0:T(8,128)(2,1)S(1)}, bf16[1,1,16,128,384]{4,3,2,1,0:T(8,128)(2,1)}, u32[]{:S(2)}) copy-start(bf16[1,1,16,128,384]{4,3,2,1,0:T(8,128)(2,1)} %param.6) | copy-start | bytes 4718596
  5.6 6.2 %copy-start.4 = (s32[2,1]{0,1:T(1,128)S(1)}, s32[2,1]{0,1:T(1,128)}, u32[]{:S(2)}) copy-start(s32[2,1]{0,1:T(1,128)} %param.7) | copy-start | bytes 28
  5.6 12.1 %copy-start.3 = (f32[3,512]{1,0:T(4,128)S(1)}, f32[3,512]{1,0:T(4,128)}, u32[]{:S(2)}) copy-start(f32[3,512]{1,0:T(4,128)} %param.5) | copy-start | bytes 18436
  5.6 24.1 %all-to-all-start = ((bf16[8,768,128]{2,1,0:T(8,128)(2,1)}), bf16[8,768,128]{2,1,0:T(8,128)(2,1)S(1)}, u32[]{:S(2)}, u32[]{:S(2)}) async-start(bf16[8,768,128]{2,1,0:T(8,128)(2,1)} %split_block.1), calls=%async_computation | async-start | bytes 3145728 | tf_op jit(solution)/shard_map/all_to_all | solution.py:217
  11.7 6.8 %copy-start.1 = (bf16[3,131072]{1,0:T(4,128)(2,1)S(1)}, bf16[3,131072]{1,0:T(4,128)(2,1)}, u32[]{:S(2)}) copy-start(bf16[3,131072]{1,0:T(4,128)(2,1)} %param.4) | copy-start | bytes 2359300
  31.4 38.9 %all-to-all-start.1 = ((bf16[16,208,128]{2,1,0:T(8,128)(2,1)}), bf16[16,208,128]{2,1,0:T(8,128)(2,1)S(1)}, u32[]{:S(2)}, u32[]{:S(2)}) async-start(bf16[16,208,128]{2,1,0:T(8,128)(2,1)} %pack.1), calls=%async_computation.1 | async-start | bytes 1703936 | tf_op jit(solution)/shard_map/all_to_all | solution.py:217
  71.1 24.6 %all-to-all-start.2 = ((bf16[16,96,128]{2,1,0:T(8,128)(2,1)}), bf16[16,96,128]{2,1,0:T(8,128)(2,1)S(1)}, u32[]{:S(2)}, u32[]{:S(2)}) async-start(bf16[16,96,128]{2,1,0:T(8,128)(2,1)} %broadcast_in_dim.9), calls=%async_computation.2 | async-start | bytes 786432 | tf_op jit(solution)/shard_map/all_to_all | solution.py:217
  81.4 4.1 %collective-permute-start = (bf16[48,4224]{1,0:T(8,128)(2,1)S(1)}, bf16[48,4224]{1,0:T(8,128)(2,1)S(1)}, u32[]{:S(2)}, u32[]{:S(2)}) collective-permute-start(bf16[48,4224]{1,0:T(8,128)(2,1)S(1)} %line_up.1.own_ref), channel_id=1, source_target_pairs={{0,1},{1,0},{2,3},{3,2},{4,5},{5,4},{6,7},{7,6},{8,9},{9,8},{10,11... | collective-permute-start | bytes 1216520 | tf_op jit(solution)/shard_map/ppermute | solution.py:235
  121.2 11.5 %copy-start.2 = (f32[32,1024]{1,0:T(8,128)}, f32[32,1024]{1,0:T(8,128)S(1)}, u32[]{:S(2)}) copy-start(f32[32,1024]{1,0:T(8,128)S(1)} %reduce_sum.9) | copy-start | bytes 393220

commit v4 on v3

--- a/solution.py
+++ b/solution.py
@@ -21,7 +21,9 @@
 RUN_ROWS = 33
 RUN = RUN_ROWS * LANES
 PIECE = TPL * CH // LANES
-SAMPLE_ROWS = 112
+HALF_ROWS = 17
+HALF = HALF_ROWS * LANES
+SAMPLE_ROWS = 64
 SEND_ROWS = STEPS * PIECE + SAMPLE_ROWS
 CHUNKS = ((0, 1152), (1152, 2176), (2176, 3200), (3200, RUN))
 LAGS = 8
@@ -34,11 +36,11 @@
 
 
 def cube_of(group):
-    return (group // 32) * HI + (group // 4) % HI
+    return ((group >> 5) << 2) | ((group >> 2) & 3)
 
 
 def class_of(group):
-    return ((group // 16) % 2) * 4 + group % 4
+    return ((group >> 2) & 4) | (group & 3)
 
 
 def group_index(cube, klass):
@@ -107,26 +109,29 @@
     )(block)
 
 
-def pack_kernel(place_ref, first_ref, second_ref, samples_ref, out_ref, wide_ref, stage_ref):
-    run = place_ref[0]
+def pack_kernel(place_ref, samples_ref, *refs):
+    *near, out_ref, wide_ref, stage_ref = refs
+    start_of_quarter = place_ref[0] * 128 + place_ref[2] * 16
     wide_ref[:, 0:1024, :] = samples_ref[...].astype(jnp.float32)
     wide_ref[:, 1024:, :] = jnp.zeros((STATION, 8, LANES), jnp.float32)
-    stage_ref[STATION * RUN_ROWS :, :] = jnp.zeros((SAMPLE_ROWS - STATION * RUN_ROWS, LANES), jnp.float32)
+    stage_ref[STATION * HALF_ROWS :, :] = jnp.zeros((SAMPLE_ROWS - STATION * HALF_ROWS, LANES), jnp.float32)
     for cube in range(CUBES):
         z_hi, y_hi = divmod(cube, HI)
-        out_ref[cube, 0:PIECE, :] = first_ref[cube * PIECE : (cube + 1) * PIECE, :]
-        out_ref[cube, PIECE : 2 * PIECE, :] = second_ref[cube * PIECE : (cube + 1) * PIECE, :]
-        start = pl.multiple_of(run * 128 + (z_hi * 256 + y_hi * 32), 32)
+        for step, near_ref in enumerate(near):
+            out_ref[cube, step * PIECE : (step + 1) * PIECE, :] = near_ref[cube * PIECE : (cube + 1) * PIECE, :]
+        if not near:
+            out_ref[cube, 0 : 2 * PIECE, :] = jnp.zeros((2 * PIECE, LANES), jnp.bfloat16)
+        start = pl.multiple_of(start_of_quarter + (z_hi * 256 + y_hi * 32), 16)
         for ch in range(STATION):
-            stage_ref[ch * RUN_ROWS : (ch + 1) * RUN_ROWS, :] = wide_ref[ch, pl.ds(start, RUN_ROWS), :]
+            stage_ref[ch * HALF_ROWS : (ch + 1) * HALF_ROWS, :] = wide_ref[ch, pl.ds(start, HALF_ROWS), :]
         out_ref[cube, 2 * PIECE :, :] = stage_ref[...].astype(jnp.bfloat16)
 
 
-def pack(place, first, second, samples):
+def pack(place, samples, *near):
     return pl.pallas_call(
         pack_kernel,
         out_shape=jax.ShapeDtypeStruct((CUBES, SEND_ROWS, LANES), jnp.bfloat16),
-        in_specs=[pl.BlockSpec(memory_space=pltpu.SMEM)] + [pl.BlockSpec(memory_space=pltpu.VMEM)] * 3,
+        in_specs=[pl.BlockSpec(memory_space=pltpu.SMEM)] + [pl.BlockSpec(memory_space=pltpu.VMEM)] * (1 + len(near)),
         out_specs=pl.BlockSpec(memory_space=pltpu.VMEM),
         scratch_shapes=[
             pltpu.VMEM((STATION, 1032, LANES), jnp.float32),
@@ -135,22 +140,22 @@
         compiler_params=vmem(8),
         cost_estimate=pl.CostEstimate(flops=1_000_000, bytes_accessed=2 << 20, transcendentals=0),
         name="pack",
-    )(place, first, second, samples)
+    )(place, samples, *near)
 
 
 def line_up_kernel(received_ref, out_ref, stage_ref):
     for cube in range(CUBES):
         stage_ref[cube * SAMPLE_ROWS : (cube + 1) * SAMPLE_ROWS, :] = received_ref[cube, 2 * PIECE :, :].astype(jnp.float32)
     for ch in range(STATION):
-        for block in range(RUN_ROWS):
-            rows = stage_ref[pl.ds(ch * RUN_ROWS + block, CUBES, stride=SAMPLE_ROWS), :]
+        for block in range(HALF_ROWS):
+            rows = stage_ref[pl.ds(ch * HALF_ROWS + block, CUBES, stride=SAMPLE_ROWS), :]
             out_ref[ch * CUBES : (ch + 1) * CUBES, block * LANES : (block + 1) * LANES] = rows.astype(jnp.bfloat16)
 
 
 def line_up(received):
     return pl.pallas_call(
         line_up_kernel,
-        out_shape=jax.ShapeDtypeStruct((CLASS_CH, RUN), jnp.bfloat16),
+        out_shape=jax.ShapeDtypeStruct((CLASS_CH, HALF), jnp.bfloat16),
         in_specs=[pl.BlockSpec(memory_space=pltpu.VMEM)],
         out_specs=pl.BlockSpec(memory_space=pltpu.VMEM),
         scratch_shapes=[pltpu.VMEM((CUBES * SAMPLE_ROWS, LANES), jnp.float32)],
@@ -158,6 +163,33 @@
         cost_estimate=pl.CostEstimate(flops=1_000_000, bytes_accessed=1 << 20, transcendentals=0),
         name="line_up",
     )(received)
+
+
+def join_kernel(place_ref, own_ref, other_ref, out_ref):
+    second = place_ref[2] == 1
+    body = HALF - LANES
+
+    @pl.when(second)
+    def _():
+        out_ref[:, 0:body] = other_ref[:, 0:body]
+        out_ref[:, body:] = own_ref[...]
+
+    @pl.when(jnp.logical_not(second))
+    def _():
+        out_ref[:, 0:body] = own_ref[:, 0:body]
+        out_ref[:, body:] = other_ref[...]
+
+
+def join(place, own, other):
+    return pl.pallas_call(
+        join_kernel,
+        out_shape=jax.ShapeDtypeStruct((CLASS_CH, RUN), jnp.bfloat16),
+        in_specs=[pl.BlockSpec(memory_space=pltpu.SMEM)] + [pl.BlockSpec(memory_space=pltpu.VMEM)] * 2,
+        out_specs=pl.BlockSpec(memory_space=pltpu.VMEM),
+        compiler_params=vmem(4),
+        cost_estimate=pl.CostEstimate(flops=1_000_000, bytes_accessed=1 << 20, transcendentals=0),
+        name="join",
+    )(place, own, other)
 
 
 def correlate_kernel(
@@ -219,19 +251,32 @@
 
 def body(traces, scales, templates, owners):
     station_ch, samples_all = traces.shape
-    place = jnp.stack([lax.axis_index("bank") % 2, class_of(lax.axis_index("group"))]).astype(jnp.int32)
-    blocked = traces.astype(jnp.float32).reshape(station_ch, scales.shape[1], -1)
-    samples = (blocked * scales[:, :, None]).astype(jnp.bfloat16).reshape(station_ch, samples_all // LANES, LANES)
-    by_class = exchange(split_block(templates[0, 0]), CUBE_GROUPS)
-    near = [lax.dynamic_index_in_dim(by_class, class_of(owners[step, 0]), 0, keepdims=False) for step in range(STEPS)]
-    received = exchange(pack(place, near[0], near[1], samples), CLASS_GROUPS)
+    group, bank = lax.axis_index("group"), lax.axis_index("bank")
+    place = jnp.stack([bank & 1, class_of(group), bank >> 1]).astype(jnp.int32)
+    owner = [owners[step, 0] for step in range(STEPS)]
+
+    def scaled():
+        blocked = traces.astype(jnp.float32).reshape(station_ch, scales.shape[1], -1)
+        samples = (blocked * scales[:, :, None]).astype(jnp.bfloat16)
+        return samples.reshape(station_ch, samples_all // LANES, LANES)
+
+    def with_blocks():
+        by_class = exchange(split_block(templates[0, 0]), CUBE_GROUPS)
+        near = [lax.dynamic_index_in_dim(by_class, class_of(owner[step]), 0, keepdims=False) for step in range(STEPS)]
+        return pack(place, scaled(), *near)
+
+    def without_blocks():
+        return pack(place, scaled())
+
+    holds_owner = (cube_of(owner[0]) == cube_of(group)) | (cube_of(owner[1]) == cube_of(group))
+    received = exchange(lax.cond(holds_owner, with_blocks, without_blocks), CLASS_GROUPS)
     far = [
-        lax.dynamic_slice(received, (cube_of(owners[step, 0]), step * PIECE, 0), (1, PIECE, LANES))
-        for step in range(STEPS)
+        lax.dynamic_slice(received, (cube_of(owner[step]), step * PIECE, 0), (1, PIECE, LANES)) for step in range(STEPS)
     ]
     piece = jnp.concatenate(far, axis=1)
     pieces = exchange(jnp.broadcast_to(piece, (CUBES, STEPS * PIECE, LANES)), CLASS_GROUPS)
-    own = line_up(received)
+    half = line_up(received)
+    own = join(place, half, lax.ppermute(half, "bank", [(0, 2), (2, 0), (1, 3), (3, 1)]))
     other = lax.ppermute(own, "bank", [(0, 1), (1, 0), (2, 3), (3, 2)])
     partial = exchange(correlate(place, pieces, own, other), CUBE_GROUPS)
     scores = jnp.sum(partial, axis=0).reshape(STEPS, 1, TPL, TIME_DEV)

time: 133 us -> 126 us (0.947)
  waiting for transfers between devices: 43 us -> 25.4 us
  starting transfers between devices: 36.7 us -> 54.2 us
  Pallas kernels: 12.2 us -> 9.12 us
  between operations: 6.22 us -> 3.19 us
    all_to_all x3 -> x2, waiting for transfers between devices: 41.7 us -> 19.8 us  [exchange(): lax.all_to_all(array, 'group', 0, 0, axis_index_groups=groups, tiled=True)]
    ppermute x0 -> x1, starting transfers between devices: none -> 12.1 us  [body(): lax.ppermute(half, 'bank', [(0, 2), (2, 0), (1, 3), (3, 1)])]
    ppermute x0 -> x1, waiting for transfers between devices: none -> 4.47 us  [body(): lax.ppermute(half, 'bank', [(0, 2), (2, 0), (1, 3), (3, 1)])]
    all_to_all x3 -> x2, starting transfers between devices: 33.9 us -> 38.4 us  [exchange(): lax.all_to_all(array, 'group', 0, 0, axis_index_groups=groups, tiled=True)]
    pallas_call x1, Pallas kernels: 3.52 us -> 0.58 us  [join(): pl.pallas_call(join_kernel, out_shape=jax.ShapeDtypeStruct((CLASS_CH, RUN...]
    unnamed x10 -> x2, local copies, waits for them, and re-layouts: 1.42 us -> 0.01 us
  transfers between devices with their start and end apart: 4 -> 4, of which waited for: 4 -> 3; matrix products, arithmetic and copies ran while one was open for 2% -> 0% of each run, Pallas kernels for 0% -> 1%
where the time goes in v4:
time: 126 us
  starting transfers between devices  54.2 us (43%)
  blocking collectives  29.4 us (23%)
  waiting for transfers between devices  25.4 us (20%)
  Pallas kernels  9.12 us (7%)
  local copies, waits for them, and re-layouts  3.67 us (3%)
  between operations  3.19 us (3%)
    all_to_all x2, starting transfers between devices, exchange(): lax.all_to_all(array, 'group', 0, 0, axis_index_groups=groups, tiled=True)  38.4 us
    all_to_all x2, waiting for transfers between devices, exchange(): lax.all_to_all(array, 'group', 0, 0, axis_index_groups=groups, tiled=True)  19.8 us
    all_to_all x1, blocking collectives, exchange(): lax.all_to_all(array, 'group', 0, 0, axis_index_groups=groups, tiled=True)  18.6 us
    ppermute x1, starting transfers between devices, body(): lax.ppermute(half, 'bank', [(0, 2), (2, 0), (1, 3), (3, 1)])  12.1 us
    pmax x1, blocking collectives, body(): best_score = lax.pmax(jnp.max(scores, axis=(0, 1, 2)), 'bank')  10.8 us
    pallas_call x1, Pallas kernels, correlate(): pl.pallas_call(correlate_kernel, out_shape=jax.ShapeDtypeStruct((CLASSES,...  6.63 us
    ppermute x1, waiting for transfers between devices, body(): lax.ppermute(half, 'bank', [(0, 2), (2, 0), (1, 3), (3, 1)])  4.47 us
    ppermute x1, starting transfers between devices, body(): other = lax.ppermute(own, 'bank', [(0, 1), (1, 0), (2, 3), (3, 2)])  3.72 us
  transfers between devices with their start and end apart: 4, of which 3 were waited for; matrix products, arithmetic and copies ran while one was open for 0% of the time, Pallas kernels for 1%

profile of v4, /device:TPU:1, one launch (start us, length us, event | category | flops | bytes accessed | tf_op | source)
XLA Modules:
  0.0 125.9 jit_solution(9557671627456125356)
XLA Ops:
  0.6 1.4 %fusion.2 = (s32[1,1]{0,1:T(1,128)}, s32[1,1]{0,1:T(1,128)}) fusion(s32[2,1]{0,1:T(1,128)} %param.9), kind=kLoop, calls=%fused_computation.12 | loop fusion | bytes 16 | tf_op jit(solution)/shard_map/slice | solution.py:256
  4.5 0.1 pad_add_fusion.place_ref
  4.6 3.9 %conditional.1 = (bf16[16,160,128]{2,1,0:T(8,128)(2,1)}) conditional(s32[]{:T(128)} %convert_element_type.13, (bf16[3,131072]{1,0:T(4,128)(2,1)}, f32[3,512]{1,0:T(4,128)}, s32[3]{0:T(128)S(1)}) %tuple.14, (bf16[3,131072]{1,0:T(4,128)(2,1)}, f32[3,512]{1,0:T(4,128)}, bf16[1,1,16,128,384]{4,3,2,1,0:T(8,128)(2,1)}, s32[]{:T(128)}, s32[]{:T(128)}, ...), branch_computations={%region_0.0_spmd, %region_1.2_spmd} | conditional | flops 1002179648 | bytes 18692364 | solution.py:272
  4.6 1.0 mul.18
  5.6 0.5 mul.19
  6.1 0.2 convert_bitcast_fusion
  6.3 0.5 fusion.samples_ref
  6.8 1.6 %pack.2 = bf16[16,160,128]{2,1,0:T(8,128)(2,1)} custom-call(s32[3]{0:T(128)S(1)} %get-tuple-element.11.place_ref, bf16[3,1024,128]{2,1,0:T(8,128)(2,1)S(1)} %fusion.samples_ref), custom_call_target="tpu_custom_call" | custom-call | flops 1000000 | bytes 2097152 | tf_op jit(solution)/shard_map/cond/branch_0_fun/pack/pallas_call | solution.py:131
  8.4 30.8 %all-to-all-start.1 = ((bf16[16,160,128]{2,1,0:T(8,128)(2,1)}), bf16[16,160,128]{2,1,0:T(8,128)(2,1)S(1)}, u32[]{:S(2)}, u32[]{:S(2)}) async-start(bf16[16,160,128]{2,1,0:T(8,128)(2,1)} %get-tuple-element.40), calls=%async_computation.1 | async-start | bytes 1310720 | tf_op jit(solution)/shard_map/all_to_all | solution.py:249
  39.3 19.8 %all-to-all-done.1.received_ref = bf16[16,160,128]{2,1,0:T(8,128)(2,1)S(1)} async-done(((bf16[16,160,128]{2,1,0:T(8,128)(2,1)}), bf16[16,160,128]{2,1,0:T(8,128)(2,1)S(1)}, u32[]{:S(2)}, u32[]{:S(2)}) %all-to-all-start.1) | async-done | bytes 655392 | tf_op jit(solution)/shard_map/all_to_all | solution.py:249
  59.1 0.8 broadcast_in_dim.10
  59.9 7.6 %all-to-all-start.2 = ((bf16[16,96,128]{2,1,0:T(8,128)(2,1)}), bf16[16,96,128]{2,1,0:T(8,128)(2,1)S(1)}, u32[]{:S(2)}, u32[]{:S(2)}) async-start(bf16[16,96,128]{2,1,0:T(8,128)(2,1)} %broadcast_in_dim.10), calls=%async_computation.2 | async-start | bytes 786432 | tf_op jit(solution)/shard_map/all_to_all | solution.py:249
  67.4 0.3 line_up.1.own_ref
  67.7 12.1 %collective-permute-start = (bf16[48,2176]{1,0:T(8,128)(2,1)S(1)}, bf16[48,2176]{1,0:T(8,128)(2,1)S(1)}, u32[]{:S(2)}, u32[]{:S(2)}) collective-permute-start(bf16[48,2176]{1,0:T(8,128)(2,1)S(1)} %line_up.1.own_ref), channel_id=1, source_target_pairs={{0,2},{2,0},{1,3},{3,1},{4,6},{6,4},{5,7},{7,5},{8,10},{10,8},{9,1... | collective-permute-start | bytes 626696 | tf_op jit(solution)/shard_map/ppermute | solution.py:279
  79.8 4.5 %collective-permute-done.other_ref = bf16[48,2176]{1,0:T(8,128)(2,1)S(1)} collective-permute-done((bf16[48,2176]{1,0:T(8,128)(2,1)S(1)}, bf16[48,2176]{1,0:T(8,128)(2,1)S(1)}, u32[]{:S(2)}, u32[]{:S(2)}) %collective-permute-start) | collective-permute-done | bytes 208928 | tf_op jit(solution)/shard_map/ppermute | solution.py:279
  84.3 0.6 join.1.own_ref
  84.9 3.7 %collective-permute-start.1 = (bf16[48,4224]{1,0:T(8,128)(2,1)S(1)}, bf16[48,4224]{1,0:T(8,128)(2,1)S(1)}, u32[]{:S(2)}, u32[]{:S(2)}) collective-permute-start(bf16[48,4224]{1,0:T(8,128)(2,1)S(1)} %join.1.own_ref), channel_id=1, source_target_pairs={{0,1},{1,0},{2,3},{3,2},{4,5},{5,4},{6,7},{7,6},{8,9},{9,8},{10,11... | collective-permute-start | bytes 1216520 | tf_op jit(solution)/shard_map/ppermute | solution.py:280
  88.6 1.2 collective-permute-done.1.other_ref
  89.8 0.0 all-to-all-done.2.pieces_ref
  89.8 6.6 %correlate.1 = f32[8,32,1024]{2,1,0:T(8,128)S(1)} custom-call(s32[3]{0:T(128)S(1)} %pad_add_fusion.place_ref, bf16[16,96,128]{2,1,0:T(8,128)(2,1)S(1)} %all-to-all-done.2.pieces_ref, bf16[48,4224]{1,0:T(8,128)(2,1)S(1)} %join.1.own_ref, bf16[48,4224]{1,0:T(8,128)(2,1)S(1)} %collective-permute-done.1.other_ref), custom_call_target="tpu_custom_call" | custom-call | flops 3400000000 | bytes 3145728 | tf_op jit(solution)/shard_map/correlate/pallas_call | solution.py:231
  96.4 18.6 %all_to_all.19 = f32[8,32,1024]{2,1,0:T(8,128)S(1)} all-to-all(f32[8,32,1024]{2,1,0:T(8,128)S(1)} %correlate.1), channel_id=1, replica_groups={{0,4,8,12,64,68,72,76},{16,20,24,28,80,84,88,92},{32,36,40,44,96,100,10..., dimensions={0} | all-to-all | bytes 2097152 | tf_op jit(solution)/shard_map/all_to_all | solution.py:249
  115.0 0.1 reduce_sum.9
  115.1 0.0 copy-start.2
  115.1 10.8 %pmax.7 = f32[1024]{0:T(1024)} all-reduce(f32[1024]{0:T(1024)S(1)} %reduce_max.9), channel_id=1, replica_groups=mesh['group'=128,'bank'=4] {'bank'}, use_global_device_ids=true, to_apply=%region_4.5 | all-reduce | flops 1024 | bytes 8192 | tf_op jit(solution)/shard_map/pmax | solution.py:283
  (6 shorter events, 0.0 us)
Async XLA Ops:
  4.6 1.5 %copy-start = (bf16[3,131072]{1,0:T(4,128)(2,1)S(1)}, bf16[3,131072]{1,0:T(4,128)(2,1)}, u32[]{:S(2)}) copy-start(bf16[3,131072]{1,0:T(4,128)(2,1)} %get-tuple-element.22) | copy-start | bytes 2359300 | tf_op jit(solution)/shard_map/cond
  8.4 50.6 %all-to-all-start.1 = ((bf16[16,160,128]{2,1,0:T(8,128)(2,1)}), bf16[16,160,128]{2,1,0:T(8,128)(2,1)S(1)}, u32[]{:S(2)}, u32[]{:S(2)}) async-start(bf16[16,160,128]{2,1,0:T(8,128)(2,1)} %get-tuple-element.40), calls=%async_computation.1 | async-start | bytes 1310720 | tf_op jit(solution)/shard_map/all_to_all | solution.py:249
  59.9 29.9 %all-to-all-start.2 = ((bf16[16,96,128]{2,1,0:T(8,128)(2,1)}), bf16[16,96,128]{2,1,0:T(8,128)(2,1)S(1)}, u32[]{:S(2)}, u32[]{:S(2)}) async-start(bf16[16,96,128]{2,1,0:T(8,128)(2,1)} %broadcast_in_dim.10), calls=%async_computation.2 | async-start | bytes 786432 | tf_op jit(solution)/shard_map/all_to_all | solution.py:249
  67.7 16.6 %collective-permute-start = (bf16[48,2176]{1,0:T(8,128)(2,1)S(1)}, bf16[48,2176]{1,0:T(8,128)(2,1)S(1)}, u32[]{:S(2)}, u32[]{:S(2)}) collective-permute-start(bf16[48,2176]{1,0:T(8,128)(2,1)S(1)} %line_up.1.own_ref), channel_id=1, source_target_pairs={{0,2},{2,0},{1,3},{3,1},{4,6},{6,4},{5,7},{7,5},{8,10},{10,8},{9,1... | collective-permute-start | bytes 626696 | tf_op jit(solution)/shard_map/ppermute | solution.py:279
  84.9 4.9 %collective-permute-start.1 = (bf16[48,4224]{1,0:T(8,128)(2,1)S(1)}, bf16[48,4224]{1,0:T(8,128)(2,1)S(1)}, u32[]{:S(2)}, u32[]{:S(2)}) collective-permute-start(bf16[48,4224]{1,0:T(8,128)(2,1)S(1)} %join.1.own_ref), channel_id=1, source_target_pairs={{0,1},{1,0},{2,3},{3,2},{4,5},{5,4},{6,7},{7,6},{8,9},{9,8},{10,11... | collective-permute-start | bytes 1216520 | tf_op jit(solution)/shard_map/ppermute | solution.py:280
  115.1 10.8 %copy-start.2 = (f32[32,1024]{1,0:T(8,128)}, f32[32,1024]{1,0:T(8,128)S(1)}, u32[]{:S(2)}) copy-start(f32[32,1024]{1,0:T(8,128)S(1)} %reduce_sum.9) | copy-start | bytes 393220

commit v5 on v3

v5 whole, which is shorter than its diff:
```python
import jax
import jax.numpy as jnp
from jax import lax
from jax.experimental import pallas as pl
from jax.experimental.pallas import tpu as pltpu
from jax.sharding import PartitionSpec as P

TLEN = 128
STEPS = 2
TPL = 16
CH = 384
TIME_DEV = 1024
LANES = 128

HI = 4
CUBES = 16
CLASSES = 8
STATION = 3
CLASS_CH = CUBES * STATION
SHIFTS = TLEN // 16
RUN_ROWS = 33
RUN = RUN_ROWS * LANES
PIECE = TPL * CH // LANES
HALF_ROWS = 17
HALF = HALF_ROWS * LANES
SAMPLE_ROWS = 64
CHUNKS = ((0, 1152), (1152, HALF))
LAGS = 8
DEPTH = TLEN // LAGS * CLASS_CH
ROWS = LAGS * STEPS * TPL


def vmem(mebibytes):
    return pltpu.CompilerParams(vmem_limit_bytes=mebibytes * 1024 * 1024)


def cube_of(group):
    return ((group >> 5) << 2) | ((group >> 2) & 3)


def class_of(group):
    return ((group >> 2) & 4) | (group & 3)


def group_index(cube, klass):
    z_hi, y_hi = divmod(cube, HI)
    z_lo, low = divmod(klass, 4)
    return z_hi * 32 + z_lo * 16 + y_hi * 4 + low


CLASS_GROUPS = [[group_index(cube, klass) for cube in range(CUBES)] for klass in range(CLASSES)]
CUBE_GROUPS = [[group_index(cube, klass) for klass in range(CLASSES)] for cube in range(CUBES)]


def iota(shape, axis):
    return lax.broadcasted_iota(jnp.int32, shape, axis)


def matmul(left, right):
    return jnp.dot(left, right, preferred_element_type=jnp.float32)


def in_hbm(array):
    return pltpu.with_memory_space_constraint(array, pltpu.HBM)


def one_hot(flags):
    return jnp.where(flags, 1.0, 0.0).astype(jnp.bfloat16)


def split_kernel(owners_ref, place_ref, block_ref, plan_ref, out_ref, rows_ref, order_ref, moved_ref, packed_ref, sems):
    loads = [
        pltpu.make_async_copy(block_ref.at[pl.ds(at, 4)], rows_ref.at[pl.ds(at, 4)], sems.at[CLASSES + at // 4])
        for at in range(0, TPL, 4)
    ]
    for load in loads:
        load.start()
    first, second, group = owners_ref[0, 0], owners_ref[0, 1], place_ref[1]
    plan_ref[1], plan_ref[2] = class_of(first), class_of(second)
    plan_ref[3], plan_ref[4] = cube_of(first), cube_of(second)
    here = cube_of(group)
    holds = jnp.where((cube_of(first) == here) | (cube_of(second) == here), 1, 0)
    plan_ref[0] = holds + jnp.where(cube_of(first) == cube_of(second), 2, 0)
    plan_ref[5] = jnp.where(cube_of(first) == here, class_of(first), class_of(second))
    channel = iota((CH, 1), 0)
    station = channel // STATION
    target = class_of(station) * CLASS_CH + (channel % STATION) * CUBES + cube_of(station)
    order_ref[...] = one_hot(iota((CH, CH), 1) == target)
    for part, load in enumerate(loads):
        load.wait()
        rows = rows_ref[part * 4 : part * 4 + 4].reshape(4 * TLEN, CH)
        sorted_rows = matmul(rows, order_ref[...]).astype(jnp.bfloat16).reshape(4, TLEN, CH)
        for shift in range(SHIFTS):
            lags = sorted_rows[:, shift * 16 : shift * 16 + 16, :].reshape(64, CH)
            moved_ref[shift, part * 64 : part * 64 + 64, :] = pltpu.roll(lags, shift * CLASS_CH, 1) if shift else lags
    copies = []
    for klass in range(CLASSES):
        for tile in range(CH // LANES):
            lanes = slice(tile * LANES, (tile + 1) * LANES)
            slot_of_lane = (iota((1, LANES), 1) + tile * LANES) // CLASS_CH
            slots = range(tile * LANES // CLASS_CH, (tile * LANES + LANES - 1) // CLASS_CH + 1)
            packed = moved_ref[(slots[0] - klass) % CLASSES, :, lanes]
            for slot in slots[1:]:
                packed = jnp.where(slot_of_lane == slot, moved_ref[(slot - klass) % CLASSES, :, lanes], packed)
            for template in range(TPL):
                at = template * PIECE + tile * 16
                packed_ref[klass, at : at + 16, :] = packed[template * 16 : template * 16 + 16]
        copies.append(pltpu.make_async_copy(packed_ref.at[klass], out_ref.at[klass], sems.at[klass]))
        copies[-1].start()
    for copy in copies:
        copy.wait()


def split_block(owners, place, block):
    return pl.pallas_call(
        split_kernel,
        out_shape=[
            jax.ShapeDtypeStruct((8,), jnp.int32),
            pltpu.HBM((CLASSES, TPL * PIECE, LANES), jnp.bfloat16),
        ],
        in_specs=[pl.BlockSpec(memory_space=pltpu.SMEM)] * 2 + [pl.BlockSpec(memory_space=pl.ANY)],
        out_specs=[pl.BlockSpec(memory_space=pltpu.SMEM), pl.BlockSpec(memory_space=pl.ANY)],
        scratch_shapes=[
            pltpu.VMEM((TPL, TLEN, CH), jnp.bfloat16),
            pltpu.VMEM((CH, CH), jnp.bfloat16),
            pltpu.VMEM((SHIFTS, TPL * 16, CH), jnp.bfloat16),
            pltpu.VMEM((CLASSES, TPL * PIECE, LANES), jnp.bfloat16),
            pltpu.SemaphoreType.DMA((CLASSES + 4,)),
        ],
        compiler_params=vmem(16),
        cost_estimate=pl.CostEstimate(flops=1_000_000_000, bytes_accessed=3 << 20, transcendentals=0),
        name="split_block",
    )(owners, place, in_hbm(block))


def pack_kernel(place_ref, samples_ref, out_ref, wide_ref, stage_ref):
    bank = place_ref[0]
    start_of_quarter = (bank & 1) * 128 + (bank >> 1) * 16
    wide_ref[:, 0:1024, :] = samples_ref[...].astype(jnp.float32)
    wide_ref[:, 1024:, :] = jnp.zeros((STATION, 8, LANES), jnp.float32)
    stage_ref[STATION * HALF_ROWS :, :] = jnp.zeros((SAMPLE_ROWS - STATION * HALF_ROWS, LANES), jnp.float32)
    for cube in range(CUBES):
        z_hi, y_hi = divmod(cube, HI)
        start = pl.multiple_of(start_of_quarter + (z_hi * 256 + y_hi * 32), 16)
        for ch in range(STATION):
            stage_ref[ch * HALF_ROWS : (ch + 1) * HALF_ROWS, :] = wide_ref[ch, pl.ds(start, HALF_ROWS), :]
        out_ref[cube] = stage_ref[...].astype(jnp.bfloat16)


def pack(place, samples):
    return pl.pallas_call(
        pack_kernel,
        out_shape=jax.ShapeDtypeStruct((CUBES, SAMPLE_ROWS, LANES), jnp.bfloat16),
        in_specs=[pl.BlockSpec(memory_space=pltpu.SMEM), pl.BlockSpec(memory_space=pltpu.VMEM)],
        out_specs=pl.BlockSpec(memory_space=pltpu.VMEM),
        scratch_shapes=[
            pltpu.VMEM((STATION, 1032, LANES), jnp.float32),
            pltpu.VMEM((SAMPLE_ROWS, LANES), jnp.float32),
        ],
        compiler_params=vmem(8),
        cost_estimate=pl.CostEstimate(flops=1_000_000, bytes_accessed=2 << 20, transcendentals=0),
        name="pack",
    )(place, samples)


def assemble_kernel(plan_ref, near_ref, rows_ref, out_ref):
    pieces = (out_ref.shape[1] - SAMPLE_ROWS) // PIECE
    for cube in range(CUBES):
        for at in range(pieces):
            out_ref[cube, at * PIECE : (at + 1) * PIECE, :] = near_ref[
                plan_ref[1 + at if pieces == STEPS else 5], cube * PIECE : (cube + 1) * PIECE, :
            ]
        out_ref[cube, pieces * PIECE :, :] = rows_ref[cube]


def assemble(pieces, plan, near, rows):
    return pl.pallas_call(
        assemble_kernel,
        out_shape=jax.ShapeDtypeStruct((CUBES, pieces * PIECE + SAMPLE_ROWS, LANES), jnp.bfloat16),
        in_specs=[pl.BlockSpec(memory_space=pltpu.SMEM)] + [pl.BlockSpec(memory_space=pltpu.VMEM)] * 2,
        out_specs=pl.BlockSpec(memory_space=pltpu.VMEM),
        compiler_params=vmem(8),
        cost_estimate=pl.CostEstimate(flops=1_000_000, bytes_accessed=2 << 20, transcendentals=0),
        name="assemble",
    )(plan, near, rows)


def line_up_kernel(plan_ref, received_ref, pieces_ref, out_ref, stage_ref):
    count = (received_ref.shape[1] - SAMPLE_ROWS) // PIECE
    for step in range(STEPS):
        at = step * PIECE if count == STEPS else 0
        piece = received_ref[plan_ref[3 + step], at : at + PIECE, :]
        for cube in range(CUBES):
            pieces_ref[cube, step * PIECE : (step + 1) * PIECE, :] = piece
    for cube in range(CUBES):
        stage_ref[cube * SAMPLE_ROWS : (cube + 1) * SAMPLE_ROWS, :] = received_ref[cube, count * PIECE :, :].astype(jnp.float32)
    for ch in range(STATION):
        for block in range(HALF_ROWS):
            rows = stage_ref[pl.ds(ch * HALF_ROWS + block, CUBES, stride=SAMPLE_ROWS), :]
            out_ref[ch * CUBES : (ch + 1) * CUBES, block * LANES : (block + 1) * LANES] = rows.astype(jnp.bfloat16)


def line_up(plan, received):
    return pl.pallas_call(
        line_up_kernel,
        out_shape=[
            jax.ShapeDtypeStruct((CUBES, STEPS * PIECE, LANES), jnp.bfloat16),
            jax.ShapeDtypeStruct((CLASS_CH, HALF), jnp.bfloat16),
        ],
        in_specs=[pl.BlockSpec(memory_space=pltpu.SMEM), pl.BlockSpec(memory_space=pltpu.VMEM)],
        out_specs=[pl.BlockSpec(memory_space=pltpu.VMEM)] * 2,
        scratch_shapes=[pltpu.VMEM((CUBES * SAMPLE_ROWS, LANES), jnp.float32)],
        compiler_params=vmem(8),
        cost_estimate=pl.CostEstimate(flops=1_000_000, bytes_accessed=2 << 20, transcendentals=0),
        name="line_up",
    )(plan, received)


def correlate_kernel(place_ref, pieces_ref, *refs):
    *lines, out_ref, natural_ref, weight_ref, moved_ref, product_ref = refs
    own_run, own_half, klass = place_ref[0] & 1, place_ref[0] >> 1, class_of(place_ref[1])
    for quarter, line_ref in enumerate(lines):
        line = line_ref[...]
        for odd in range(2):
            for shift in range(SHIFTS):
                by = 16 * shift + 8 * odd
                at = odd * CH + shift * CLASS_CH
                moved_ref[quarter, at : at + CLASS_CH, :] = pltpu.roll(line, HALF - by, 1) if by else line
    for template in range(TPL):
        for step in range(STEPS):
            row = (template * STEPS + step) * 16
            for tile in range(CH // LANES):
                at = step * PIECE + tile * 16
                natural_ref[row : row + 16, tile * LANES : (tile + 1) * LANES] = pieces_ref[template, at : at + 16, :]
    wanted = iota((2 * ROWS, 1), 0)
    lag, step, template = wanted // 32, (wanted // 16) % 2, wanted % 16
    order = one_hot(iota((2 * ROWS, 2 * ROWS), 1) == (template * 2 + step) * 16 + lag)
    ordered = pltpu.roll(matmul(order, natural_ref[...]), (CH - klass * CLASS_CH) % CH, 1).astype(jnp.bfloat16)
    weight_ref[:, 0:CH] = ordered[0:ROWS]
    weight_ref[:, CH:] = ordered[ROWS:]
    for quarter in range(4):
        first = (own_run ^ (quarter >> 1)) * 4 + (own_half ^ (quarter & 1)) * 2
        for part, (start, stop) in enumerate(CHUNKS):
            product_ref[quarter, :, start:stop] = matmul(weight_ref[...], moved_ref[quarter, :, start:stop])
            at = part * TIME_DEV
            total = product_ref[quarter, 0:32, at : at + TIME_DEV]
            for lag in range(1, LAGS):
                window = product_ref[quarter, lag * 32 : (lag + 1) * 32, at : at + TIME_DEV + LANES]
                total = total + pltpu.roll(window, TIME_DEV + LANES - lag, 1)[:, :TIME_DEV]
            out_ref[first + part] = total


def correlate(place, pieces, *lines):
    return pl.pallas_call(
        correlate_kernel,
        out_shape=jax.ShapeDtypeStruct((CLASSES, STEPS * TPL, TIME_DEV), jnp.float32),
        in_specs=[pl.BlockSpec(memory_space=pltpu.SMEM)] + [pl.BlockSpec(memory_space=pltpu.VMEM)] * 5,
        out_specs=pl.BlockSpec(memory_space=pltpu.VMEM),
        scratch_shapes=[
            pltpu.VMEM((2 * ROWS, CH), jnp.bfloat16),
            pltpu.VMEM((ROWS, DEPTH), jnp.bfloat16),
            pltpu.VMEM((4, DEPTH, HALF), jnp.bfloat16),
            pltpu.VMEM((4, ROWS, HALF), jnp.float32),
        ],
        compiler_params=vmem(32),
        cost_estimate=pl.CostEstimate(flops=3_400_000_000, bytes_accessed=3 << 20, transcendentals=0),
        name="correlate",
    )(place, pieces, *lines)


def exchange(array, groups):
    return lax.all_to_all(array, "group", 0, 0, axis_index_groups=groups, tiled=True)


def body(traces, scales, templates, owners):
    station_ch, samples_all = traces.shape
    place = jnp.stack([lax.axis_index("bank"), lax.axis_index("group")]).astype(jnp.int32)
    plan, by_class = split_block(owners.T, place, templates[0, 0])

    def sample_rows():
        blocked = traces.astype(jnp.float32).reshape(station_ch, scales.shape[1], -1)
        samples = (blocked * scales[:, :, None]).astype(jnp.bfloat16)
        return pack(place, samples.reshape(station_ch, samples_all // LANES, LANES))

    holds_owner, one_cube = (plan[0] & 1) == 1, plan[0] >= 2

    def from_cubes(count):
        def with_blocks():
            return assemble(count, plan, exchange(by_class, CUBE_GROUPS), sample_rows())

        def without_blocks():
            return jnp.pad(sample_rows(), ((0, 0), (count * PIECE, 0), (0, 0)))

        return line_up(plan, exchange(lax.cond(holds_owner, with_blocks, without_blocks), CLASS_GROUPS))

    piece, own = lax.cond(one_cube, lambda: from_cubes(2), lambda: from_cubes(1))
    halves, cores = [(0, 2), (2, 0), (1, 3), (3, 1)], [(0, 1), (1, 0), (2, 3), (3, 2)]
    other = lax.ppermute(own, "bank", halves)
    lines = [own, other, lax.ppermute(own, "bank", cores), lax.ppermute(other, "bank", cores)]
    pieces = exchange(piece, CLASS_GROUPS)
    partial = exchange(correlate(place, pieces, *lines), CUBE_GROUPS)
    scores = jnp.sum(partial, axis=0).reshape(STEPS, 1, TPL, TIME_DEV)
    best_score = lax.pmax(jnp.max(scores, axis=(0, 1, 2)), "bank")
    return (scores, best_score)


def solution(mesh):
    placed = (
        P("group", None),
        P("group", None),
        P("bank", "group", None, None, None),
        P(None, "bank"),
    )
    return jax.shard_map(
        body,
        mesh=mesh,
        in_specs=placed,
        out_specs=(P(None, "bank", None, "group"), P("group")),
        check_vma=False,
    )
```

time: 133 us -> 113 us (0.85)
  waiting for transfers between devices: 43 us -> 12.4 us
  blocking collectives: 30.2 us -> 49 us
  starting transfers between devices: 36.7 us -> 31.2 us
  between operations: 6.22 us -> 0.8 us
  Pallas kernels: 12.2 us -> 16.3 us
  local copies, waits for them, and re-layouts: 3.55 us -> 1.38 us
    all_to_all x3 -> x2, waiting for transfers between devices: 41.7 us -> 11 us  [exchange(): lax.all_to_all(array, 'group', 0, 0, axis_index_groups=groups, tiled=True)]
    all_to_all x3 -> x2, starting transfers between devices: 33.9 us -> 10 us  [exchange(): lax.all_to_all(array, 'group', 0, 0, axis_index_groups=groups, tiled=True)]
    all_to_all x1 -> x2, blocking collectives: 18.8 us -> 38.3 us  [exchange(): lax.all_to_all(array, 'group', 0, 0, axis_index_groups=groups, tiled=True)]
    ppermute x1 -> x3, starting transfers between devices: 2.71 us -> 21.2 us  [the longest x1 13.4 us: body(): other = lax.ppermute(own, 'bank', halves)]
    pallas_call x3 -> x4, Pallas kernels: 5.52 us -> 9.2 us  [the longest x1 5.55 us: split_block(): pl.pallas_call(split_kernel, out_shape=[jax.ShapeDtypeStruct((8,), jnp.in...]
  transfers between devices with their start and end apart: 4 -> 5, of which waited for: 4 -> 3; matrix products, arithmetic and copies ran while one was open for 2% -> 1% of each run, Pallas kernels for 0% -> 1%
where the time goes in v5:
time: 113 us; the launch traced here: 112 us
  blocking collectives  49 us (43%)
  starting transfers between devices  31.2 us (28%)
  Pallas kernels  16.3 us (14%)
  waiting for transfers between devices  12.4 us (11%)
  local copies, waits for them, and re-layouts  1.38 us (1%)
    all_to_all x2, blocking collectives, exchange(): lax.all_to_all(array, 'group', 0, 0, axis_index_groups=groups, tiled=True)  38.3 us
    ppermute x1, starting transfers between devices, body(): other = lax.ppermute(own, 'bank', halves)  13.4 us
    all_to_all x2, waiting for transfers between devices, exchange(): lax.all_to_all(array, 'group', 0, 0, axis_index_groups=groups, tiled=True)  11 us
    pmax x1, blocking collectives, body(): best_score = lax.pmax(jnp.max(scores, axis=(0, 1, 2)), 'bank')  10.7 us
    all_to_all x2, starting transfers between devices, exchange(): lax.all_to_all(array, 'group', 0, 0, axis_index_groups=groups, tiled=True)  10 us
    pallas_call x1, Pallas kernels, correlate(): pl.pallas_call(correlate_kernel, out_shape=jax.ShapeDtypeStruct((CLASSES,...  7.13 us
    pallas_call x1, Pallas kernels, split_block(): pl.pallas_call(split_kernel, out_shape=[jax.ShapeDtypeStruct((8,), jnp.in...  5.55 us
    ppermute x1, starting transfers between devices, body(): lax.ppermute(other, 'bank', cores)  4.18 us
  transfers between devices with their start and end apart: 5, of which 3 were waited for; matrix products, arithmetic and copies ran while one was open for 1% of the time, Pallas kernels for 1%

profile of v5, /device:TPU:1, one launch (start us, length us, event | category | flops | bytes accessed | tf_op | source)
XLA Modules:
  0.0 112.0 jit_solution(21854470163390840)
XLA Ops:
  0.6 0.1 pad_add_fusion.place_ref
  0.7 0.7 copy-done
  1.4 5.6 %split_block.1 = (s32[8]{0:T(128)S(1)}, bf16[8,768,128]{2,1,0:T(8,128)(2,1)}) custom-call(s32[1,2]{1,0:T(1,128)S(1)} %bitcast.32, s32[2]{0:T(128)S(1)} %pad_add_fusion.place_ref, bf16[16,128,384]{2,1,0:T(8,128)(2,1)} %bitcast.36), custom_call_target="tpu_custom_call" | custom-call | flops 1000000000 | bytes 3145728 | tf_op jit(solution)/shard_map/split_block/pallas_call | solution.py:115
  7.0 43.3 %conditional.3 = ((bf16[16,96,128]{2,1,0:T(8,128)(2,1)}, bf16[48,2176]{1,0:T(8,128)(2,1)})) conditional(s32[]{:T(128)} %bitcast.4, (pred[]{:T(512)}, bf16[3,131072]{1,0:T(4,128)(2,1)S(1)}, f32[3,512]{1,0:T(4,128)S(1)}, s32[2]{0:T(128)S(1)}, bf16[8,768,128]{2,1,0:T(8,128)(2,1)}, /*index=5*/s32[8]{0:T(128)S(1)}) %tuple.38, (pred[]{:T(512)}, ...), branch_computations={%region_0.3_spmd, %region_3.6_spmd} | conditional | flops 4179649 | bytes 17094772 | solution.py:296
  7.0 20.7 %conditional = (bf16[16,112,128]{2,1,0:T(8,128)(2,1)}) conditional(s32[]{:T(128)} %convert_element_type.30, (bf16[3,131072]{1,0:T(4,128)(2,1)S(1)}, f32[3,512]{1,0:T(4,128)S(1)}, s32[2]{0:T(128)S(1)}) %tuple.18, (bf16[8,768,128]{2,1,0:T(8,128)(2,1)}, bf16[3,131072]{1,0:T(4,128)(2,1)S(1)}, f32[3,512]{1,0:T(4,128)S(1)}, s32[2]{0:T(128)S(1)}, ...), branch_computations={%region_1.1_spmd, %region_2.2_spmd} | conditional | flops 3179648 | bytes 13686824 | solution.py:294
  7.1 6.2 %all-to-all-start = ((bf16[8,768,128]{2,1,0:T(8,128)(2,1)}), bf16[8,768,128]{2,1,0:T(8,128)(2,1)S(1)}, u32[]{:S(2)}, u32[]{:S(2)}) async-start(bf16[8,768,128]{2,1,0:T(8,128)(2,1)} %get-tuple-element.66), calls=%async_computation | async-start | bytes 3145728 | tf_op jit(solution)/shard_map/cond/branch_0_fun/cond/branch_1_fun/all_to_all | solution.py:272
  13.2 0.3 mul.40
  13.5 0.5 mul.41
  13.9 0.2 convert_bitcast_fusion.1
  14.2 0.5 fusion.1.samples_ref
  14.6 0.7 pack.5.rows_ref
  15.4 11.0 %all-to-all-done.near_ref = bf16[8,768,128]{2,1,0:T(8,128)(2,1)S(1)} async-done(((bf16[8,768,128]{2,1,0:T(8,128)(2,1)}), bf16[8,768,128]{2,1,0:T(8,128)(2,1)S(1)}, u32[]{:S(2)}, u32[]{:S(2)}) %all-to-all-start) | async-done | bytes 1572896 | tf_op jit(solution)/shard_map/cond/branch_0_fun/cond/branch_1_fun/all_to_all | solution.py:272
  26.3 1.3 %assemble.2 = bf16[16,112,128]{2,1,0:T(8,128)(2,1)} custom-call(s32[8]{0:T(128)S(1)} %get-tuple-element.65.plan_ref, bf16[8,768,128]{2,1,0:T(8,128)(2,1)S(1)} %all-to-all-done.near_ref, bf16[16,64,128]{2,1,0:T(8,128)(2,1)S(1)} %pack.5.rows_ref), custom_call_target="tpu_custom_call" | custom-call | flops 1000000 | bytes 2097152 | tf_op jit(solution)/shard_map/cond/branch_0_fun/cond/branch_1_fun/assemble/pallas_call | solution.py:177
  27.7 21.1 %all_to_all.26.received_ref = bf16[16,112,128]{2,1,0:T(8,128)(2,1)S(1)} all-to-all(bf16[16,112,128]{2,1,0:T(8,128)(2,1)} %get-tuple-element.104), channel_id=1, replica_groups={{0,16,32,48,128,144,160,176,256,272,288,304,384,400,416,432},{4,20,36,5..., dimensions={0} | all-to-all | bytes 917504 | tf_op jit(solution)/shard_map/cond/branch_0_fun/all_to_all | solution.py:272
  48.8 1.6 %line_up.2 = (bf16[16,96,128]{2,1,0:T(8,128)(2,1)}, bf16[48,2176]{1,0:T(8,128)(2,1)}) custom-call(s32[8]{0:T(128)S(1)} %get-tuple-element.70.plan_ref, bf16[16,112,128]{2,1,0:T(8,128)(2,1)S(1)} %all_to_all.26.received_ref), custom_call_target="tpu_custom_call" | custom-call | flops 1000000 | bytes 2097152 | tf_op jit(solution)/shard_map/cond/branch_0_fun/line_up/pallas_call | solution.py:204
  50.3 3.9 %all-to-all-start.4 = ((bf16[16,96,128]{2,1,0:T(8,128)(2,1)}), bf16[16,96,128]{2,1,0:T(8,128)(2,1)S(1)}, u32[]{:S(2)}, u32[]{:S(2)}) async-start(bf16[16,96,128]{2,1,0:T(8,128)(2,1)} %get-tuple-element.98), calls=%async_computation.4 | async-start | bytes 786432 | tf_op jit(solution)/shard_map/all_to_all | solution.py:272
  54.2 13.4 %collective-permute-start = (bf16[48,2176]{1,0:T(8,128)(2,1)}, bf16[48,2176]{1,0:T(8,128)(2,1)S(1)}, u32[]{:S(2)}, u32[]{:S(2)}) collective-permute-start(bf16[48,2176]{1,0:T(8,128)(2,1)} %get-tuple-element.99.refs_0_), channel_id=1, source_target_pairs={{0,2},{2,0},{1,3},{3,1},{4,6},{6,4},{5,7},{7,5},{8,10},{10,8},{9,1... | collective-permute-start | bytes 626696 | tf_op jit(solution)/shard_map/ppermute | solution.py:298
  67.6 3.6 %collective-permute-start.1 = (bf16[48,2176]{1,0:T(8,128)(2,1)}, bf16[48,2176]{1,0:T(8,128)(2,1)S(1)}, u32[]{:S(2)}, u32[]{:S(2)}) collective-permute-start(bf16[48,2176]{1,0:T(8,128)(2,1)} %get-tuple-element.99.refs_0_), channel_id=1, source_target_pairs={{0,1},{1,0},{2,3},{3,2},{4,5},{5,4},{6,7},{7,6},{8,9},{9,8},{10,11... | collective-permute-start | bytes 626696 | tf_op jit(solution)/shard_map/ppermute | solution.py:299
  71.2 0.6 collective-permute-done.refs_1_
  71.8 4.2 %collective-permute-start.2 = (bf16[48,2176]{1,0:T(8,128)(2,1)S(1)}, bf16[48,2176]{1,0:T(8,128)(2,1)S(1)}, u32[]{:S(2)}, u32[]{:S(2)}) collective-permute-start(bf16[48,2176]{1,0:T(8,128)(2,1)S(1)} %collective-permute-done.refs_1_), channel_id=1, source_target_pairs={{0,1},{1,0},{2,3},{3,2},{4,5},{5,4},{6,7},{7,6},{8,9},{9,8},{10,11... | collective-permute-start | bytes 626696 | tf_op jit(solution)/shard_map/ppermute | solution.py:299
  76.0 0.9 collective-permute-done.2.refs_3_
  76.9 7.1 %correlate.1 = f32[8,32,1024]{2,1,0:T(8,128)S(1)} custom-call(s32[2]{0:T(128)S(1)} %pad_add_fusion.place_ref, bf16[16,96,128]{2,1,0:T(8,128)(2,1)S(1)} %all-to-all-done.4.pieces_ref, bf16[48,2176]{1,0:T(8,128)(2,1)} %get-tuple-element.99.refs_0_, bf16[48,2176]{1,0:T(8,128)(2,1)S(1)} %collective-permute-done.refs_1_, ...), custom_call_target="tpu_custom_call" | custom-call | flops 3400000000 | bytes 3145728 | tf_op jit(solution)/shard_map/correlate/pallas_call | solution.py:254
  84.0 17.2 %all_to_all.28 = f32[8,32,1024]{2,1,0:T(8,128)S(1)} all-to-all(f32[8,32,1024]{2,1,0:T(8,128)S(1)} %correlate.1), channel_id=1, replica_groups={{0,4,8,12,64,68,72,76},{16,20,24,28,80,84,88,92},{32,36,40,44,96,100,10..., dimensions={0} | all-to-all | bytes 2097152 | tf_op jit(solution)/shard_map/all_to_all | solution.py:272
  101.3 10.7 %pmax.7 = f32[1024]{0:T(1024)} all-reduce(f32[1024]{0:T(1024)S(1)} %reduce_max.9), channel_id=1, replica_groups=mesh['group'=128,'bank'=4] {'bank'}, use_global_device_ids=true, to_apply=%region_8.9 | all-reduce | flops 1024 | bytes 8192 | tf_op jit(solution)/shard_map/pmax | solution.py:303
  (11 shorter events, 0.1 us)
Async XLA Ops:
  0.7 0.7 copy-start
  1.4 5.6 %copy-start.1 = (bf16[3,131072]{1,0:T(4,128)(2,1)S(1)}, bf16[3,131072]{1,0:T(4,128)(2,1)}, u32[]{:S(2)}) copy-start(bf16[3,131072]{1,0:T(4,128)(2,1)} %param.10) | copy-start | bytes 2359300
  1.4 5.6 %copy-start.3 = (f32[3,512]{1,0:T(4,128)S(1)}, f32[3,512]{1,0:T(4,128)}, u32[]{:S(2)}) copy-start(f32[3,512]{1,0:T(4,128)} %param.11) | copy-start | bytes 18436
  7.1 19.3 %all-to-all-start = ((bf16[8,768,128]{2,1,0:T(8,128)(2,1)}), bf16[8,768,128]{2,1,0:T(8,128)(2,1)S(1)}, u32[]{:S(2)}, u32[]{:S(2)}) async-start(bf16[8,768,128]{2,1,0:T(8,128)(2,1)} %get-tuple-element.66), calls=%async_computation | async-start | bytes 3145728 | tf_op jit(solution)/shard_map/cond/branch_0_fun/cond/branch_1_fun/all_to_all | solution.py:272
  50.3 26.5 %all-to-all-start.4 = ((bf16[16,96,128]{2,1,0:T(8,128)(2,1)}), bf16[16,96,128]{2,1,0:T(8,128)(2,1)S(1)}, u32[]{:S(2)}, u32[]{:S(2)}) async-start(bf16[16,96,128]{2,1,0:T(8,128)(2,1)} %get-tuple-element.98), calls=%async_computation.4 | async-start | bytes 786432 | tf_op jit(solution)/shard_map/all_to_all | solution.py:272
  54.2 17.6 %collective-permute-start = (bf16[48,2176]{1,0:T(8,128)(2,1)}, bf16[48,2176]{1,0:T(8,128)(2,1)S(1)}, u32[]{:S(2)}, u32[]{:S(2)}) collective-permute-start(bf16[48,2176]{1,0:T(8,128)(2,1)} %get-tuple-element.99.refs_0_), channel_id=1, source_target_pairs={{0,2},{2,0},{1,3},{3,1},{4,6},{6,4},{5,7},{7,5},{8,10},{10,8},{9,1... | collective-permute-start | bytes 626696 | tf_op jit(solution)/shard_map/ppermute | solution.py:298
  67.6 8.4 %collective-permute-start.1 = (bf16[48,2176]{1,0:T(8,128)(2,1)}, bf16[48,2176]{1,0:T(8,128)(2,1)S(1)}, u32[]{:S(2)}, u32[]{:S(2)}) collective-permute-start(bf16[48,2176]{1,0:T(8,128)(2,1)} %get-tuple-element.99.refs_0_), channel_id=1, source_target_pairs={{0,1},{1,0},{2,3},{3,2},{4,5},{5,4},{6,7},{7,6},{8,9},{9,8},{10,11... | collective-permute-start | bytes 626696 | tf_op jit(solution)/shard_map/ppermute | solution.py:299
  71.8 5.1 %collective-permute-start.2 = (bf16[48,2176]{1,0:T(8,128)(2,1)S(1)}, bf16[48,2176]{1,0:T(8,128)(2,1)S(1)}, u32[]{:S(2)}, u32[]{:S(2)}) collective-permute-start(bf16[48,2176]{1,0:T(8,128)(2,1)S(1)} %collective-permute-done.refs_1_), channel_id=1, source_target_pairs={{0,1},{1,0},{2,3},{3,2},{4,5},{5,4},{6,7},{7,6},{8,9},{9,8},{10,11... | collective-permute-start | bytes 626696 | tf_op jit(solution)/shard_map/ppermute | solution.py:299
  101.3 10.7 %copy-start.2 = (f32[32,1024]{1,0:T(8,128)}, f32[32,1024]{1,0:T(8,128)S(1)}, u32[]{:S(2)}) copy-start(f32[32,1024]{1,0:T(8,128)S(1)} %reduce_sum.9) | copy-start | bytes 393220

commit v6 on v5

--- a/solution.py
+++ b/solution.py
@@ -68,14 +68,20 @@
     return jnp.where(flags, 1.0, 0.0).astype(jnp.bfloat16)
 
 
-def split_kernel(owners_ref, place_ref, block_ref, plan_ref, out_ref, rows_ref, order_ref, moved_ref, packed_ref, sems):
+def split_kernel(
+    owners_ref, block_ref, plan_ref, out_ref, owner_ref, rows_ref, order_ref, moved_ref, packed_ref, sems
+):
     loads = [
         pltpu.make_async_copy(block_ref.at[pl.ds(at, 4)], rows_ref.at[pl.ds(at, 4)], sems.at[CLASSES + at // 4])
         for at in range(0, TPL, 4)
     ]
     for load in loads:
         load.start()
-    first, second, group = owners_ref[0, 0], owners_ref[0, 1], place_ref[1]
+    group = lax.axis_index("group")
+    read = pltpu.make_async_copy(owners_ref, owner_ref, sems.at[CLASSES + 4])
+    read.start()
+    read.wait()
+    first, second = owner_ref[0, 0], owner_ref[0, 1]
     plan_ref[1], plan_ref[2] = class_of(first), class_of(second)
     plan_ref[3], plan_ref[4] = cube_of(first), cube_of(second)
     here = cube_of(group)
@@ -111,30 +117,31 @@
         copy.wait()
 
 
-def split_block(owners, place, block):
+def split_block(owners, block):
     return pl.pallas_call(
         split_kernel,
         out_shape=[
             jax.ShapeDtypeStruct((8,), jnp.int32),
             pltpu.HBM((CLASSES, TPL * PIECE, LANES), jnp.bfloat16),
         ],
-        in_specs=[pl.BlockSpec(memory_space=pltpu.SMEM)] * 2 + [pl.BlockSpec(memory_space=pl.ANY)],
+        in_specs=[pl.BlockSpec(memory_space=pl.ANY)] * 2,
         out_specs=[pl.BlockSpec(memory_space=pltpu.SMEM), pl.BlockSpec(memory_space=pl.ANY)],
         scratch_shapes=[
+            pltpu.SMEM((1, STEPS), jnp.int32),
             pltpu.VMEM((TPL, TLEN, CH), jnp.bfloat16),
             pltpu.VMEM((CH, CH), jnp.bfloat16),
             pltpu.VMEM((SHIFTS, TPL * 16, CH), jnp.bfloat16),
             pltpu.VMEM((CLASSES, TPL * PIECE, LANES), jnp.bfloat16),
-            pltpu.SemaphoreType.DMA((CLASSES + 4,)),
+            pltpu.SemaphoreType.DMA((CLASSES + 5,)),
         ],
         compiler_params=vmem(16),
         cost_estimate=pl.CostEstimate(flops=1_000_000_000, bytes_accessed=3 << 20, transcendentals=0),
         name="split_block",
-    )(owners, place, in_hbm(block))
-
-
-def pack_kernel(place_ref, samples_ref, out_ref, wide_ref, stage_ref):
-    bank = place_ref[0]
+    )(in_hbm(owners), in_hbm(block))
+
+
+def pack_kernel(samples_ref, out_ref, wide_ref, stage_ref):
+    bank = lax.axis_index("bank")
     start_of_quarter = (bank & 1) * 128 + (bank >> 1) * 16
     wide_ref[:, 0:1024, :] = samples_ref[...].astype(jnp.float32)
     wide_ref[:, 1024:, :] = jnp.zeros((STATION, 8, LANES), jnp.float32)
@@ -147,11 +154,11 @@
         out_ref[cube] = stage_ref[...].astype(jnp.bfloat16)
 
 
-def pack(place, samples):
+def pack(samples):
     return pl.pallas_call(
         pack_kernel,
         out_shape=jax.ShapeDtypeStruct((CUBES, SAMPLE_ROWS, LANES), jnp.bfloat16),
-        in_specs=[pl.BlockSpec(memory_space=pltpu.SMEM), pl.BlockSpec(memory_space=pltpu.VMEM)],
+        in_specs=[pl.BlockSpec(memory_space=pltpu.VMEM)],
         out_specs=pl.BlockSpec(memory_space=pltpu.VMEM),
         scratch_shapes=[
             pltpu.VMEM((STATION, 1032, LANES), jnp.float32),
@@ -160,7 +167,7 @@
         compiler_params=vmem(8),
         cost_estimate=pl.CostEstimate(flops=1_000_000, bytes_accessed=2 << 20, transcendentals=0),
         name="pack",
-    )(place, samples)
+    )(samples)
 
 
 def assemble_kernel(plan_ref, near_ref, rows_ref, out_ref):
@@ -216,9 +223,10 @@
     )(plan, received)
 
 
-def correlate_kernel(place_ref, pieces_ref, *refs):
+def correlate_kernel(pieces_ref, *refs):
     *lines, out_ref, natural_ref, weight_ref, moved_ref, product_ref = refs
-    own_run, own_half, klass = place_ref[0] & 1, place_ref[0] >> 1, class_of(place_ref[1])
+    bank = lax.axis_index("bank")
+    own_run, own_half, klass = bank & 1, bank >> 1, class_of(lax.axis_index("group"))
     for quarter, line_ref in enumerate(lines):
         line = line_ref[...]
         for odd in range(2):
@@ -250,11 +258,11 @@
             out_ref[first + part] = total
 
 
-def correlate(place, pieces, *lines):
+def correlate(pieces, *lines):
     return pl.pallas_call(
         correlate_kernel,
         out_shape=jax.ShapeDtypeStruct((CLASSES, STEPS * TPL, TIME_DEV), jnp.float32),
-        in_specs=[pl.BlockSpec(memory_space=pltpu.SMEM)] + [pl.BlockSpec(memory_space=pltpu.VMEM)] * 5,
+        in_specs=[pl.BlockSpec(memory_space=pltpu.VMEM)] * 5,
         out_specs=pl.BlockSpec(memory_space=pltpu.VMEM),
         scratch_shapes=[
             pltpu.VMEM((2 * ROWS, CH), jnp.bfloat16),
@@ -265,7 +273,7 @@
         compiler_params=vmem(32),
         cost_estimate=pl.CostEstimate(flops=3_400_000_000, bytes_accessed=3 << 20, transcendentals=0),
         name="correlate",
-    )(place, pieces, *lines)
+    )(pieces, *lines)
 
 
 def exchange(array, groups):
@@ -274,13 +282,12 @@
 
 def body(traces, scales, templates, owners):
     station_ch, samples_all = traces.shape
-    place = jnp.stack([lax.axis_index("bank"), lax.axis_index("group")]).astype(jnp.int32)
-    plan, by_class = split_block(owners.T, place, templates[0, 0])
+    plan, by_class = split_block(owners.T, templates[0, 0])
 
     def sample_rows():
         blocked = traces.astype(jnp.float32).reshape(station_ch, scales.shape[1], -1)
         samples = (blocked * scales[:, :, None]).astype(jnp.bfloat16)
-        return pack(place, samples.reshape(station_ch, samples_all // LANES, LANES))
+        return pack(samples.reshape(station_ch, samples_all // LANES, LANES))
 
     holds_owner, one_cube = (plan[0] & 1) == 1, plan[0] >= 2
 
@@ -298,7 +305,7 @@
     other = lax.ppermute(own, "bank", halves)
     lines = [own, other, lax.ppermute(own, "bank", cores), lax.ppermute(other, "bank", cores)]
     pieces = exchange(piece, CLASS_GROUPS)
-    partial = exchange(correlate(place, pieces, *lines), CUBE_GROUPS)
+    partial = exchange(correlate(pieces, *lines), CUBE_GROUPS)
     scores = jnp.sum(partial, axis=0).reshape(STEPS, 1, TPL, TIME_DEV)
     best_score = lax.pmax(jnp.max(scores, axis=(0, 1, 2)), "bank")
     return (scores, best_score)

time: 113 us -> 110 us (0.973)
  starting transfers between devices: 31.2 us -> 27.7 us
  blocking collectives: 49 us -> 50.8 us
    ppermute x1, starting transfers between devices: 13.4 us -> 1.92 us  [body(): other = lax.ppermute(own, 'bank', halves)]
    ppermute x1, starting transfers between devices: 3.65 us -> 9.08 us  [body(): lax.ppermute(own, 'bank', cores)]
    all_to_all x2, blocking collectives: 38.3 us -> 40.7 us  [exchange(): lax.all_to_all(array, 'group', 0, 0, axis_index_groups=groups, tiled=True)]
    ppermute x1, starting transfers between devices: 4.18 us -> 6.46 us  [body(): lax.ppermute(other, 'bank', cores)]
  transfers between devices with their start and end apart: 5 -> 5, of which waited for: 3 -> 2; matrix products, arithmetic and copies ran while one was open for 1% -> 1% of each run, Pallas kernels for 1% -> 0%
where the time goes in v6:
time: 110 us; the launch traced here: 109 us
  blocking collectives  50.8 us (46%)
  starting transfers between devices  27.7 us (25%)
  Pallas kernels  15.4 us (14%)
  waiting for transfers between devices  12.4 us (11%)
    all_to_all x2, blocking collectives, exchange(): lax.all_to_all(array, 'group', 0, 0, axis_index_groups=groups, tiled=True)  40.7 us
    all_to_all x2, waiting for transfers between devices, exchange(): lax.all_to_all(array, 'group', 0, 0, axis_index_groups=groups, tiled=True)  11.5 us
    all_to_all x2, starting transfers between devices, exchange(): lax.all_to_all(array, 'group', 0, 0, axis_index_groups=groups, tiled=True)  10.3 us
    pmax x1, blocking collectives, body(): best_score = lax.pmax(jnp.max(scores, axis=(0, 1, 2)), 'bank')  10.1 us
    ppermute x1, starting transfers between devices, body(): lax.ppermute(own, 'bank', cores)  9.08 us
    pallas_call x1, Pallas kernels, correlate(): pl.pallas_call(correlate_kernel, out_shape=jax.ShapeDtypeStruct((CLASSES,...  7.12 us
    ppermute x1, starting transfers between devices, body(): lax.ppermute(other, 'bank', cores)  6.46 us
    pallas_call x1, Pallas kernels, split_block(): pl.pallas_call(split_kernel, out_shape=[jax.ShapeDtypeStruct((8,), jnp.in...  5.11 us
  transfers between devices with their start and end apart: 5, of which 2 were waited for; matrix products, arithmetic and copies ran while one was open for 1% of the time, Pallas kernels for 0%

profile of v6, /device:TPU:1, one launch (start us, length us, event | category | flops | bytes accessed | tf_op | source)
XLA Modules:
  0.0 108.7 jit_solution(7778390012004728442)
XLA Ops:
  0.7 5.1 %split_block.1 = (s32[8]{0:T(128)S(1)}, bf16[8,768,128]{2,1,0:T(8,128)(2,1)}) custom-call(s32[1,2]{1,0:T(1,128)} %bitcast.34, bf16[16,128,384]{2,1,0:T(8,128)(2,1)} %bitcast.33), custom_call_target="tpu_custom_call" | custom-call | flops 1000000000 | bytes 3145728 | tf_op jit(solution)/shard_map/split_block/pallas_call | solution.py:121
  5.9 47.2 %conditional.3 = ((bf16[16,96,128]{2,1,0:T(8,128)(2,1)}, bf16[48,2176]{1,0:T(8,128)(2,1)})) conditional(s32[]{:T(128)} %bitcast.2, (pred[]{:T(512)}, bf16[3,131072]{1,0:T(4,128)(2,1)S(1)}, f32[3,512]{1,0:T(4,128)S(1)}, bf16[8,768,128]{2,1,0:T(8,128)(2,1)}, s32[8]{0:T(128)S(1)}) %tuple.38, (pred[]{:T(512)}, bf16[3,131072]{1,0:T(4,128)(2,1)S(1)}, ...), branch_computations={%region_0.3_spmd, %region_3.6_spmd} | conditional | flops 4179649 | bytes 17094756 | solution.py:303
  5.9 20.7 %conditional = (bf16[16,112,128]{2,1,0:T(8,128)(2,1)}) conditional(s32[]{:T(128)} %convert_element_type.30, (bf16[3,131072]{1,0:T(4,128)(2,1)S(1)}, f32[3,512]{1,0:T(4,128)S(1)}) %tuple.18, (bf16[8,768,128]{2,1,0:T(8,128)(2,1)}, bf16[3,131072]{1,0:T(4,128)(2,1)S(1)}, f32[3,512]{1,0:T(4,128)S(1)}, s32[8]{0:T(128)S(1)}) %tuple.19), branch_computations={%region_1.1_spmd, %region_2.2_spmd} | conditional | flops 3179648 | bytes 13686824 | solution.py:301
  5.9 6.2 %all-to-all-start = ((bf16[8,768,128]{2,1,0:T(8,128)(2,1)}), bf16[8,768,128]{2,1,0:T(8,128)(2,1)S(1)}, u32[]{:S(2)}, u32[]{:S(2)}) async-start(bf16[8,768,128]{2,1,0:T(8,128)(2,1)} %get-tuple-element.53), calls=%async_computation | async-start | bytes 3145728 | tf_op jit(solution)/shard_map/cond/branch_0_fun/cond/branch_1_fun/all_to_all | solution.py:280
  12.0 0.3 mul.40
  12.3 0.5 mul.41
  12.8 0.2 convert_bitcast_fusion.1
  13.0 0.5 fusion.1.samples_ref
  13.5 0.2 pack.5.rows_ref
  13.7 11.5 %all-to-all-done.near_ref = bf16[8,768,128]{2,1,0:T(8,128)(2,1)S(1)} async-done(((bf16[8,768,128]{2,1,0:T(8,128)(2,1)}), bf16[8,768,128]{2,1,0:T(8,128)(2,1)S(1)}, u32[]{:S(2)}, u32[]{:S(2)}) %all-to-all-start) | async-done | bytes 1572896 | tf_op jit(solution)/shard_map/cond/branch_0_fun/cond/branch_1_fun/all_to_all | solution.py:280
  25.2 1.4 %assemble.2 = bf16[16,112,128]{2,1,0:T(8,128)(2,1)} custom-call(s32[8]{0:T(128)S(1)} %get-tuple-element.52.plan_ref, bf16[8,768,128]{2,1,0:T(8,128)(2,1)S(1)} %all-to-all-done.near_ref, bf16[16,64,128]{2,1,0:T(8,128)(2,1)S(1)} %pack.5.rows_ref), custom_call_target="tpu_custom_call" | custom-call | flops 1000000 | bytes 2097152 | tf_op jit(solution)/shard_map/cond/branch_0_fun/cond/branch_1_fun/assemble/pallas_call | solution.py:184
  26.5 24.9 %all_to_all.26.received_ref = bf16[16,112,128]{2,1,0:T(8,128)(2,1)S(1)} all-to-all(bf16[16,112,128]{2,1,0:T(8,128)(2,1)} %get-tuple-element.86), channel_id=1, replica_groups={{0,16,32,48,128,144,160,176,256,272,288,304,384,400,416,432},{4,20,36,5..., dimensions={0} | all-to-all | bytes 917504 | tf_op jit(solution)/shard_map/cond/branch_0_fun/all_to_all | solution.py:280
  51.5 1.6 %line_up.2 = (bf16[16,96,128]{2,1,0:T(8,128)(2,1)}, bf16[48,2176]{1,0:T(8,128)(2,1)}) custom-call(s32[8]{0:T(128)S(1)} %get-tuple-element.56.plan_ref, bf16[16,112,128]{2,1,0:T(8,128)(2,1)S(1)} %all_to_all.26.received_ref), custom_call_target="tpu_custom_call" | custom-call | flops 1000000 | bytes 2097152 | tf_op jit(solution)/shard_map/cond/branch_0_fun/line_up/pallas_call | solution.py:211
  53.0 4.1 %all-to-all-start.4 = ((bf16[16,96,128]{2,1,0:T(8,128)(2,1)}), bf16[16,96,128]{2,1,0:T(8,128)(2,1)S(1)}, u32[]{:S(2)}, u32[]{:S(2)}) async-start(bf16[16,96,128]{2,1,0:T(8,128)(2,1)} %get-tuple-element.80), calls=%async_computation.4 | async-start | bytes 786432 | tf_op jit(solution)/shard_map/all_to_all | solution.py:280
  57.2 1.9 %collective-permute-start = (bf16[48,2176]{1,0:T(8,128)(2,1)}, bf16[48,2176]{1,0:T(8,128)(2,1)S(1)}, u32[]{:S(2)}, u32[]{:S(2)}) collective-permute-start(bf16[48,2176]{1,0:T(8,128)(2,1)} %get-tuple-element.81.refs_0_), channel_id=1, source_target_pairs={{0,2},{2,0},{1,3},{3,1},{4,6},{6,4},{5,7},{7,5},{8,10},{10,8},{9,1... | collective-permute-start | bytes 626696 | tf_op jit(solution)/shard_map/ppermute | solution.py:305
  59.1 9.1 %collective-permute-start.1 = (bf16[48,2176]{1,0:T(8,128)(2,1)}, bf16[48,2176]{1,0:T(8,128)(2,1)S(1)}, u32[]{:S(2)}, u32[]{:S(2)}) collective-permute-start(bf16[48,2176]{1,0:T(8,128)(2,1)} %get-tuple-element.81.refs_0_), channel_id=1, source_target_pairs={{0,1},{1,0},{2,3},{3,2},{4,5},{5,4},{6,7},{7,6},{8,9},{9,8},{10,11... | collective-permute-start | bytes 626696 | tf_op jit(solution)/shard_map/ppermute | solution.py:306
  68.2 0.0 collective-permute-done.refs_1_
  68.2 6.5 %collective-permute-start.2 = (bf16[48,2176]{1,0:T(8,128)(2,1)S(1)}, bf16[48,2176]{1,0:T(8,128)(2,1)S(1)}, u32[]{:S(2)}, u32[]{:S(2)}) collective-permute-start(bf16[48,2176]{1,0:T(8,128)(2,1)S(1)} %collective-permute-done.refs_1_), channel_id=1, source_target_pairs={{0,1},{1,0},{2,3},{3,2},{4,5},{5,4},{6,7},{7,6},{8,9},{9,8},{10,11... | collective-permute-start | bytes 626696 | tf_op jit(solution)/shard_map/ppermute | solution.py:306
  74.7 0.9 collective-permute-done.2.refs_3_
  75.5 7.1 %correlate.1 = f32[8,32,1024]{2,1,0:T(8,128)S(1)} custom-call(bf16[16,96,128]{2,1,0:T(8,128)(2,1)S(1)} %all-to-all-done.4.pieces_ref, bf16[48,2176]{1,0:T(8,128)(2,1)} %get-tuple-element.81.refs_0_, bf16[48,2176]{1,0:T(8,128)(2,1)S(1)} %collective-permute-done.refs_1_, bf16[48,2176]{1,0:T(8,128)(2,1)S(1)} %collective-permute-done.1.refs_2_, ...), custom_call_target="tpu_custom_call" | custom-call | flops 3400000000 | bytes 3145728 | tf_op jit(solution)/shard_map/correlate/pallas_call | solution.py:262
  82.7 15.8 %all_to_all.28 = f32[8,32,1024]{2,1,0:T(8,128)S(1)} all-to-all(f32[8,32,1024]{2,1,0:T(8,128)S(1)} %correlate.1), channel_id=1, replica_groups={{0,4,8,12,64,68,72,76},{16,20,24,28,80,84,88,92},{32,36,40,44,96,100,10..., dimensions={0} | all-to-all | bytes 2097152 | tf_op jit(solution)/shard_map/all_to_all | solution.py:280
  98.4 0.1 reduce_sum.9
  98.5 0.0 copy-start.1
  98.5 10.1 %pmax.7 = f32[1024]{0:T(1024)} all-reduce(f32[1024]{0:T(1024)S(1)} %reduce_max.9), channel_id=1, replica_groups=mesh['group'=128,'bank'=4] {'bank'}, use_global_device_ids=true, to_apply=%region_8.9 | all-reduce | flops 1024 | bytes 8192 | tf_op jit(solution)/shard_map/pmax | solution.py:310
  (8 shorter events, 0.0 us)
Async XLA Ops:
  0.6 5.2 %copy-start = (bf16[3,131072]{1,0:T(4,128)(2,1)S(1)}, bf16[3,131072]{1,0:T(4,128)(2,1)}, u32[]{:S(2)}) copy-start(bf16[3,131072]{1,0:T(4,128)(2,1)} %param.10) | copy-start | bytes 2359300
  0.6 5.2 %copy-start.2 = (f32[3,512]{1,0:T(4,128)S(1)}, f32[3,512]{1,0:T(4,128)}, u32[]{:S(2)}) copy-start(f32[3,512]{1,0:T(4,128)} %param.11) | copy-start | bytes 18436
  5.9 19.3 %all-to-all-start = ((bf16[8,768,128]{2,1,0:T(8,128)(2,1)}), bf16[8,768,128]{2,1,0:T(8,128)(2,1)S(1)}, u32[]{:S(2)}, u32[]{:S(2)}) async-start(bf16[8,768,128]{2,1,0:T(8,128)(2,1)} %get-tuple-element.53), calls=%async_computation | async-start | bytes 3145728 | tf_op jit(solution)/shard_map/cond/branch_0_fun/cond/branch_1_fun/all_to_all | solution.py:280
  53.0 22.5 %all-to-all-start.4 = ((bf16[16,96,128]{2,1,0:T(8,128)(2,1)}), bf16[16,96,128]{2,1,0:T(8,128)(2,1)S(1)}, u32[]{:S(2)}, u32[]{:S(2)}) async-start(bf16[16,96,128]{2,1,0:T(8,128)(2,1)} %get-tuple-element.80), calls=%async_computation.4 | async-start | bytes 786432 | tf_op jit(solution)/shard_map/all_to_all | solution.py:280
  57.2 11.0 %collective-permute-start = (bf16[48,2176]{1,0:T(8,128)(2,1)}, bf16[48,2176]{1,0:T(8,128)(2,1)S(1)}, u32[]{:S(2)}, u32[]{:S(2)}) collective-permute-start(bf16[48,2176]{1,0:T(8,128)(2,1)} %get-tuple-element.81.refs_0_), channel_id=1, source_target_pairs={{0,2},{2,0},{1,3},{3,1},{4,6},{6,4},{5,7},{7,5},{8,10},{10,8},{9,1... | collective-permute-start | bytes 626696 | tf_op jit(solution)/shard_map/ppermute | solution.py:305
  59.1 15.6 %collective-permute-start.1 = (bf16[48,2176]{1,0:T(8,128)(2,1)}, bf16[48,2176]{1,0:T(8,128)(2,1)S(1)}, u32[]{:S(2)}, u32[]{:S(2)}) collective-permute-start(bf16[48,2176]{1,0:T(8,128)(2,1)} %get-tuple-element.81.refs_0_), channel_id=1, source_target_pairs={{0,1},{1,0},{2,3},{3,2},{4,5},{5,4},{6,7},{7,6},{8,9},{9,8},{10,11... | collective-permute-start | bytes 626696 | tf_op jit(solution)/shard_map/ppermute | solution.py:306
  68.2 7.4 %collective-permute-start.2 = (bf16[48,2176]{1,0:T(8,128)(2,1)S(1)}, bf16[48,2176]{1,0:T(8,128)(2,1)S(1)}, u32[]{:S(2)}, u32[]{:S(2)}) collective-permute-start(bf16[48,2176]{1,0:T(8,128)(2,1)S(1)} %collective-permute-done.refs_1_), channel_id=1, source_target_pairs={{0,1},{1,0},{2,3},{3,2},{4,5},{5,4},{6,7},{7,6},{8,9},{9,8},{10,11... | collective-permute-start | bytes 626696 | tf_op jit(solution)/shard_map/ppermute | solution.py:306
  98.5 10.2 %copy-start.1 = (f32[32,1024]{1,0:T(8,128)}, f32[32,1024]{1,0:T(8,128)S(1)}, u32[]{:S(2)}) copy-start(f32[32,1024]{1,0:T(8,128)S(1)} %reduce_sum.9) | copy-start | bytes 393220

commit v7 on v6

--- a/solution.py
+++ b/solution.py
@@ -192,31 +192,38 @@
     )(plan, near, rows)
 
 
-def line_up_kernel(plan_ref, received_ref, pieces_ref, out_ref, stage_ref):
+def line_up_kernel(plan_ref, received_ref, pieces_ref, out_ref, copies_ref, stage_ref, sem):
     count = (received_ref.shape[1] - SAMPLE_ROWS) // PIECE
     for step in range(STEPS):
         at = step * PIECE if count == STEPS else 0
         piece = received_ref[plan_ref[3 + step], at : at + PIECE, :]
         for cube in range(CUBES):
-            pieces_ref[cube, step * PIECE : (step + 1) * PIECE, :] = piece
+            copies_ref[cube, step * PIECE : (step + 1) * PIECE, :] = piece
+    send = pltpu.make_async_copy(copies_ref, pieces_ref, sem)
+    send.start()
     for cube in range(CUBES):
         stage_ref[cube * SAMPLE_ROWS : (cube + 1) * SAMPLE_ROWS, :] = received_ref[cube, count * PIECE :, :].astype(jnp.float32)
     for ch in range(STATION):
         for block in range(HALF_ROWS):
             rows = stage_ref[pl.ds(ch * HALF_ROWS + block, CUBES, stride=SAMPLE_ROWS), :]
             out_ref[ch * CUBES : (ch + 1) * CUBES, block * LANES : (block + 1) * LANES] = rows.astype(jnp.bfloat16)
+    send.wait()
 
 
 def line_up(plan, received):
     return pl.pallas_call(
         line_up_kernel,
         out_shape=[
-            jax.ShapeDtypeStruct((CUBES, STEPS * PIECE, LANES), jnp.bfloat16),
+            pltpu.HBM((CUBES, STEPS * PIECE, LANES), jnp.bfloat16),
             jax.ShapeDtypeStruct((CLASS_CH, HALF), jnp.bfloat16),
         ],
         in_specs=[pl.BlockSpec(memory_space=pltpu.SMEM), pl.BlockSpec(memory_space=pltpu.VMEM)],
-        out_specs=[pl.BlockSpec(memory_space=pltpu.VMEM)] * 2,
-        scratch_shapes=[pltpu.VMEM((CUBES * SAMPLE_ROWS, LANES), jnp.float32)],
+        out_specs=[pl.BlockSpec(memory_space=pl.ANY), pl.BlockSpec(memory_space=pltpu.VMEM)],
+        scratch_shapes=[
+            pltpu.VMEM((CUBES, STEPS * PIECE, LANES), jnp.bfloat16),
+            pltpu.VMEM((CUBES * SAMPLE_ROWS, LANES), jnp.float32),
+            pltpu.SemaphoreType.DMA,
+        ],
         compiler_params=vmem(8),
         cost_estimate=pl.CostEstimate(flops=1_000_000, bytes_accessed=2 << 20, transcendentals=0),
         name="line_up",

time: 110 us -> 114 us (1.036); the launches traced: 109 us -> 114 us
  starting transfers between devices: 27.7 us -> 34.1 us
  blocking collectives: 50.8 us -> 48.4 us
    ppermute x1, starting transfers between devices: 1.92 us -> 16.9 us  [body(): other = lax.ppermute(own, 'bank', halves)]
    ppermute x1, starting transfers between devices: 9.08 us -> 3.36 us  [body(): lax.ppermute(own, 'bank', cores)]
    all_to_all x2, blocking collectives: 40.7 us -> 37 us  [exchange(): lax.all_to_all(array, 'group', 0, 0, axis_index_groups=groups, tiled=True)]
    ppermute x1, starting transfers between devices: 6.46 us -> 3.87 us  [body(): lax.ppermute(other, 'bank', cores)]
    pmax x1, blocking collectives: 10.1 us -> 11.4 us  [body(): best_score = lax.pmax(jnp.max(scores, axis=(0, 1, 2)), 'bank')]
    ppermute x1, waiting for transfers between devices: 0.01 us -> 1.16 us  [body(): other = lax.ppermute(own, 'bank', halves)]
  transfers between devices with their start and end apart: 5 -> 5, of which waited for: 2 -> 3; matrix products, arithmetic and copies ran while one was open for 1% -> 1% of each run, Pallas kernels for 0% -> 0%
where the time goes in v7:
time: 114 us
  blocking collectives  48.4 us (42%)
  starting transfers between devices  34.1 us (30%)
  Pallas kernels  15.9 us (14%)
  waiting for transfers between devices  13.5 us (12%)
    all_to_all x2, blocking collectives, exchange(): lax.all_to_all(array, 'group', 0, 0, axis_index_groups=groups, tiled=True)  37 us
    ppermute x1, starting transfers between devices, body(): other = lax.ppermute(own, 'bank', halves)  16.9 us
    all_to_all x2, waiting for transfers between devices, exchange(): lax.all_to_all(array, 'group', 0, 0, axis_index_groups=groups, tiled=True)  11.5 us
    pmax x1, blocking collectives, body(): best_score = lax.pmax(jnp.max(scores, axis=(0, 1, 2)), 'bank')  11.4 us
    all_to_all x2, starting transfers between devices, exchange(): lax.all_to_all(array, 'group', 0, 0, axis_index_groups=groups, tiled=True)  10 us
    pallas_call x1, Pallas kernels, correlate(): pl.pallas_call(correlate_kernel, out_shape=jax.ShapeDtypeStruct((CLASSES,...  7.12 us
    pallas_call x1, Pallas kernels, split_block(): pl.pallas_call(split_kernel, out_shape=[jax.ShapeDtypeStruct((8,), jnp.in...  5.11 us
    ppermute x1, starting transfers between devices, body(): lax.ppermute(other, 'bank', cores)  3.87 us
  transfers between devices with their start and end apart: 5, of which 3 were waited for; matrix products, arithmetic and copies ran while one was open for 1% of the time, Pallas kernels for 0%

profile of v7, /device:TPU:1, one launch (start us, length us, event | category | flops | bytes accessed | tf_op | source)
XLA Modules:
  0.0 114.4 jit_solution(6290153874312546370)
XLA Ops:
  0.7 5.1 %split_block.1 = (s32[8]{0:T(128)S(1)}, bf16[8,768,128]{2,1,0:T(8,128)(2,1)}) custom-call(s32[1,2]{1,0:T(1,128)} %bitcast.34, bf16[16,128,384]{2,1,0:T(8,128)(2,1)} %bitcast.33), custom_call_target="tpu_custom_call" | custom-call | flops 1000000000 | bytes 3145728 | tf_op jit(solution)/shard_map/split_block/pallas_call | solution.py:121
  5.9 42.5 %conditional.3 = ((bf16[16,96,128]{2,1,0:T(8,128)(2,1)}, bf16[48,2176]{1,0:T(8,128)(2,1)})) conditional(s32[]{:T(128)} %bitcast.2, (pred[]{:T(512)}, bf16[3,131072]{1,0:T(4,128)(2,1)S(1)}, f32[3,512]{1,0:T(4,128)S(1)}, bf16[8,768,128]{2,1,0:T(8,128)(2,1)}, s32[8]{0:T(128)S(1)}) %tuple.38, (pred[]{:T(512)}, bf16[3,131072]{1,0:T(4,128)(2,1)S(1)}, ...), branch_computations={%region_0.3_spmd, %region_3.6_spmd} | conditional | flops 4179649 | bytes 17094756 | solution.py:310
  5.9 20.7 %conditional.1 = (bf16[16,160,128]{2,1,0:T(8,128)(2,1)}) conditional(s32[]{:T(128)} %convert_element_type.33, (bf16[3,131072]{1,0:T(4,128)(2,1)S(1)}, f32[3,512]{1,0:T(4,128)S(1)}) %tuple.20, (bf16[8,768,128]{2,1,0:T(8,128)(2,1)}, bf16[3,131072]{1,0:T(4,128)(2,1)S(1)}, f32[3,512]{1,0:T(4,128)S(1)}, s32[8]{0:T(128)S(1)}) %tuple.21), branch_computations={%region_4.4_spmd, %region_5.5_spmd} | conditional | flops 3179648 | bytes 13686824 | solution.py:308
  5.9 6.2 %all-to-all-start.2 = ((bf16[8,768,128]{2,1,0:T(8,128)(2,1)}), bf16[8,768,128]{2,1,0:T(8,128)(2,1)S(1)}, u32[]{:S(2)}, u32[]{:S(2)}) async-start(bf16[8,768,128]{2,1,0:T(8,128)(2,1)} %get-tuple-element.64), calls=%async_computation.2 | async-start | bytes 3145728 | tf_op jit(solution)/shard_map/cond/branch_1_fun/cond/branch_1_fun/all_to_all | solution.py:287
  12.1 0.3 mul.48
  12.3 0.5 mul.49
  12.8 0.2 convert_bitcast_fusion.3
  13.0 0.5 fusion.3.samples_ref
  13.5 0.2 pack.7.rows_ref
  13.7 11.5 %all-to-all-done.2.near_ref = bf16[8,768,128]{2,1,0:T(8,128)(2,1)S(1)} async-done(((bf16[8,768,128]{2,1,0:T(8,128)(2,1)}), bf16[8,768,128]{2,1,0:T(8,128)(2,1)S(1)}, u32[]{:S(2)}, u32[]{:S(2)}) %all-to-all-start.2) | async-done | bytes 1572896 | tf_op jit(solution)/shard_map/cond/branch_1_fun/cond/branch_1_fun/all_to_all | solution.py:287
  25.2 1.4 %assemble.3 = bf16[16,160,128]{2,1,0:T(8,128)(2,1)} custom-call(s32[8]{0:T(128)S(1)} %get-tuple-element.63.plan_ref, bf16[8,768,128]{2,1,0:T(8,128)(2,1)S(1)} %all-to-all-done.2.near_ref, bf16[16,64,128]{2,1,0:T(8,128)(2,1)S(1)} %pack.7.rows_ref), custom_call_target="tpu_custom_call" | custom-call | flops 1000000 | bytes 2097152 | tf_op jit(solution)/shard_map/cond/branch_1_fun/cond/branch_1_fun/assemble/pallas_call | solution.py:184
  26.6 19.7 %all_to_all.27.received_ref = bf16[16,160,128]{2,1,0:T(8,128)(2,1)S(1)} all-to-all(bf16[16,160,128]{2,1,0:T(8,128)(2,1)} %get-tuple-element.87), channel_id=1, replica_groups={{0,16,32,48,128,144,160,176,256,272,288,304,384,400,416,432},{4,20,36,5..., dimensions={0} | all-to-all | bytes 1310720 | tf_op jit(solution)/shard_map/cond/branch_1_fun/all_to_all | solution.py:287
  46.3 2.0 %line_up.3 = (bf16[16,96,128]{2,1,0:T(8,128)(2,1)}, bf16[48,2176]{1,0:T(8,128)(2,1)}) custom-call(s32[8]{0:T(128)S(1)} %get-tuple-element.67.plan_ref, bf16[16,160,128]{2,1,0:T(8,128)(2,1)S(1)} %all_to_all.27.received_ref), custom_call_target="tpu_custom_call" | custom-call | flops 1000000 | bytes 2097152 | tf_op jit(solution)/shard_map/cond/branch_1_fun/line_up/pallas_call | solution.py:214
  48.4 3.9 %all-to-all-start.4 = ((bf16[16,96,128]{2,1,0:T(8,128)(2,1)}), bf16[16,96,128]{2,1,0:T(8,128)(2,1)S(1)}, u32[]{:S(2)}, u32[]{:S(2)}) async-start(bf16[16,96,128]{2,1,0:T(8,128)(2,1)} %get-tuple-element.80), calls=%async_computation.4 | async-start | bytes 786432 | tf_op jit(solution)/shard_map/all_to_all | solution.py:287
  52.3 16.9 %collective-permute-start = (bf16[48,2176]{1,0:T(8,128)(2,1)}, bf16[48,2176]{1,0:T(8,128)(2,1)S(1)}, u32[]{:S(2)}, u32[]{:S(2)}) collective-permute-start(bf16[48,2176]{1,0:T(8,128)(2,1)} %get-tuple-element.81.refs_0_), channel_id=1, source_target_pairs={{0,2},{2,0},{1,3},{3,1},{4,6},{6,4},{5,7},{7,5},{8,10},{10,8},{9,1... | collective-permute-start | bytes 626696 | tf_op jit(solution)/shard_map/ppermute | solution.py:312
  69.2 3.4 %collective-permute-start.1 = (bf16[48,2176]{1,0:T(8,128)(2,1)}, bf16[48,2176]{1,0:T(8,128)(2,1)S(1)}, u32[]{:S(2)}, u32[]{:S(2)}) collective-permute-start(bf16[48,2176]{1,0:T(8,128)(2,1)} %get-tuple-element.81.refs_0_), channel_id=1, source_target_pairs={{0,1},{1,0},{2,3},{3,2},{4,5},{5,4},{6,7},{7,6},{8,9},{9,8},{10,11... | collective-permute-start | bytes 626696 | tf_op jit(solution)/shard_map/ppermute | solution.py:313
  72.5 1.2 %collective-permute-done.refs_1_ = bf16[48,2176]{1,0:T(8,128)(2,1)S(1)} collective-permute-done((bf16[48,2176]{1,0:T(8,128)(2,1)}, bf16[48,2176]{1,0:T(8,128)(2,1)S(1)}, u32[]{:S(2)}, u32[]{:S(2)}) %collective-permute-start) | collective-permute-done | bytes 208928 | tf_op jit(solution)/shard_map/ppermute | solution.py:312
  73.7 3.9 %collective-permute-start.2 = (bf16[48,2176]{1,0:T(8,128)(2,1)S(1)}, bf16[48,2176]{1,0:T(8,128)(2,1)S(1)}, u32[]{:S(2)}, u32[]{:S(2)}) collective-permute-start(bf16[48,2176]{1,0:T(8,128)(2,1)S(1)} %collective-permute-done.refs_1_), channel_id=1, source_target_pairs={{0,1},{1,0},{2,3},{3,2},{4,5},{5,4},{6,7},{7,6},{8,9},{9,8},{10,11... | collective-permute-start | bytes 626696 | tf_op jit(solution)/shard_map/ppermute | solution.py:313
  77.6 0.9 collective-permute-done.2.refs_3_
  78.5 7.1 %correlate.1 = f32[8,32,1024]{2,1,0:T(8,128)S(1)} custom-call(bf16[16,96,128]{2,1,0:T(8,128)(2,1)S(1)} %all-to-all-done.4.pieces_ref, bf16[48,2176]{1,0:T(8,128)(2,1)} %get-tuple-element.81.refs_0_, bf16[48,2176]{1,0:T(8,128)(2,1)S(1)} %collective-permute-done.refs_1_, bf16[48,2176]{1,0:T(8,128)(2,1)S(1)} %collective-permute-done.1.refs_2_, ...), custom_call_target="tpu_custom_call" | custom-call | flops 3400000000 | bytes 3145728 | tf_op jit(solution)/shard_map/correlate/pallas_call | solution.py:269
  85.6 17.3 %all_to_all.28 = f32[8,32,1024]{2,1,0:T(8,128)S(1)} all-to-all(f32[8,32,1024]{2,1,0:T(8,128)S(1)} %correlate.1), channel_id=1, replica_groups={{0,4,8,12,64,68,72,76},{16,20,24,28,80,84,88,92},{32,36,40,44,96,100,10..., dimensions={0} | all-to-all | bytes 2097152 | tf_op jit(solution)/shard_map/all_to_all | solution.py:287
  102.9 0.1 reduce_sum.9
  102.9 0.0 copy-start.1
  103.0 11.4 %pmax.7 = f32[1024]{0:T(1024)} all-reduce(f32[1024]{0:T(1024)S(1)} %reduce_max.9), channel_id=1, replica_groups=mesh['group'=128,'bank'=4] {'bank'}, use_global_device_ids=true, to_apply=%region_8.9 | all-reduce | flops 1024 | bytes 8192 | tf_op jit(solution)/shard_map/pmax | solution.py:317
  (8 shorter events, 0.0 us)
Async XLA Ops:
  0.6 5.2 %copy-start = (bf16[3,131072]{1,0:T(4,128)(2,1)S(1)}, bf16[3,131072]{1,0:T(4,128)(2,1)}, u32[]{:S(2)}) copy-start(bf16[3,131072]{1,0:T(4,128)(2,1)} %param.10) | copy-start | bytes 2359300
  0.6 5.2 %copy-start.2 = (f32[3,512]{1,0:T(4,128)S(1)}, f32[3,512]{1,0:T(4,128)}, u32[]{:S(2)}) copy-start(f32[3,512]{1,0:T(4,128)} %param.11) | copy-start | bytes 18436
  5.9 19.3 %all-to-all-start.2 = ((bf16[8,768,128]{2,1,0:T(8,128)(2,1)}), bf16[8,768,128]{2,1,0:T(8,128)(2,1)S(1)}, u32[]{:S(2)}, u32[]{:S(2)}) async-start(bf16[8,768,128]{2,1,0:T(8,128)(2,1)} %get-tuple-element.64), calls=%async_computation.2 | async-start | bytes 3145728 | tf_op jit(solution)/shard_map/cond/branch_1_fun/cond/branch_1_fun/all_to_all | solution.py:287
  48.4 30.1 %all-to-all-start.4 = ((bf16[16,96,128]{2,1,0:T(8,128)(2,1)}), bf16[16,96,128]{2,1,0:T(8,128)(2,1)S(1)}, u32[]{:S(2)}, u32[]{:S(2)}) async-start(bf16[16,96,128]{2,1,0:T(8,128)(2,1)} %get-tuple-element.80), calls=%async_computation.4 | async-start | bytes 786432 | tf_op jit(solution)/shard_map/all_to_all | solution.py:287
  52.3 21.4 %collective-permute-start = (bf16[48,2176]{1,0:T(8,128)(2,1)}, bf16[48,2176]{1,0:T(8,128)(2,1)S(1)}, u32[]{:S(2)}, u32[]{:S(2)}) collective-permute-start(bf16[48,2176]{1,0:T(8,128)(2,1)} %get-tuple-element.81.refs_0_), channel_id=1, source_target_pairs={{0,2},{2,0},{1,3},{3,1},{4,6},{6,4},{5,7},{7,5},{8,10},{10,8},{9,1... | collective-permute-start | bytes 626696 | tf_op jit(solution)/shard_map/ppermute | solution.py:312
  69.2 8.4 %collective-permute-start.1 = (bf16[48,2176]{1,0:T(8,128)(2,1)}, bf16[48,2176]{1,0:T(8,128)(2,1)S(1)}, u32[]{:S(2)}, u32[]{:S(2)}) collective-permute-start(bf16[48,2176]{1,0:T(8,128)(2,1)} %get-tuple-element.81.refs_0_), channel_id=1, source_target_pairs={{0,1},{1,0},{2,3},{3,2},{4,5},{5,4},{6,7},{7,6},{8,9},{9,8},{10,11... | collective-permute-start | bytes 626696 | tf_op jit(solution)/shard_map/ppermute | solution.py:313
  73.7 4.8 %collective-permute-start.2 = (bf16[48,2176]{1,0:T(8,128)(2,1)S(1)}, bf16[48,2176]{1,0:T(8,128)(2,1)S(1)}, u32[]{:S(2)}, u32[]{:S(2)}) collective-permute-start(bf16[48,2176]{1,0:T(8,128)(2,1)S(1)} %collective-permute-done.refs_1_), channel_id=1, source_target_pairs={{0,1},{1,0},{2,3},{3,2},{4,5},{5,4},{6,7},{7,6},{8,9},{9,8},{10,11... | collective-permute-start | bytes 626696 | tf_op jit(solution)/shard_map/ppermute | solution.py:313
  102.9 11.5 %copy-start.1 = (f32[32,1024]{1,0:T(8,128)}, f32[32,1024]{1,0:T(8,128)S(1)}, u32[]{:S(2)}) copy-start(f32[32,1024]{1,0:T(8,128)S(1)} %reduce_sum.9) | copy-start | bytes 393220
